TPU v7x, 128 devices: a whole 4x4x4 slice. The times are simulated.
128 devices in a mesh: section: 2 (over core), seq: 16 (over z, y), wshard: 4 (over x).
Axes of the slice: x: 4, y: 4, z: 4, core: 2. Of those that a mesh axis runs over, the one named last changes fastest.
Arguments:
- hidden: bfloat16 [8, 2048, 1024], P('wshard', 'seq'), may hold values from -6 to 6
- out_grad: bfloat16 [8, 2048, 1024], P('wshard', 'seq'), may hold values from -6 to 6
- norm_gain: float32 [2, 1024], P('section'), may hold values from 0.1 to 1.9
- in_weight: bfloat16 [2, 1024, 4384], P('section', 'wshard'), may hold values from -0.1875 to 0.1875
- conv_weight: float32 [2, 4, 2304], P('section'), may hold values from -3 to 3
- conv_bias: float32 [2, 2304], P('section'), may hold values from -3 to 3
- dt_bias: float32 [2, 32], P('section'), may hold values from -7 to -3
- a_log: float32 [2, 32], P('section'), may hold values from -1 to 2
- d_skip: float32 [2, 32], P('section'), may hold values from -4 to 4
- out_gain: float32 [2, 2048], P('section'), may hold values from 0.1 to 1.9
- out_weight: bfloat16 [2, 2048, 1024], P('section', 'wshard'), may hold values from -0.125 to 0.125
Outputs:
- layer_out: bfloat16 [2, 8, 2048, 1024], P('section', 'wshard', 'seq')
- section_grad: float32 [2, 8, 2048, 1024], P('section', 'wshard', 'seq')
- grad_norm_gain: float32 [2, 1024], P('section')
- grad_in_weight: float32 [2, 1024, 4384], P('section', 'wshard')
- grad_conv_weight: float32 [2, 4, 2304], P('section')
- grad_conv_bias: float32 [2, 2304], P('section')
- grad_dt_bias: float32 [2, 32], P('section')
- grad_a_log: float32 [2, 32], P('section')
- grad_d_skip: float32 [2, 32], P('section')
- grad_out_gain: float32 [2, 2048], P('section')
- grad_out_weight: float32 [2, 2048, 1024], P('section', 'wshard')
All inputs are finite; a program needn't handle non-finite values.
Results may differ from a plain program's by a relative error of at most 0.022.
Values may be sent and summed in bfloat16 or wider, within the bound.
A program may use at most 192 MiB of HBM per device.

v0:
```python
import jax
import jax.numpy as jnp
from jax import lax
from jax.sharding import PartitionSpec as P

HDIM = 64
SPAN = 256


epsilon = 1e-05
highest = lax.Precision.HIGHEST


def from_behind(x, axis, by):
    devices = lax.axis_size(axis)
    pairs = [(i, i + by) for i in range(devices) if 0 <= i + by < devices]
    return lax.ppermute(x, axis, pairs)


def rms_scale(values, gain):
    return values * lax.rsqrt(jnp.mean(values * values, axis=-1, keepdims=True) + epsilon) * gain


def scan_blocks(x_conv, step_size, decay_rates, b_conv, c_conv):
    length, head_count, head_width = x_conv.shape
    states = b_conv.shape[1]
    blocks = length // SPAN
    x_blocks = x_conv.reshape(blocks, SPAN, head_count, head_width)
    step_blocks = step_size.reshape(blocks, SPAN, head_count)
    b_blocks = b_conv.reshape(blocks, SPAN, states)
    c_blocks = c_conv.reshape(blocks, SPAN, states)
    row_ids = jnp.arange(SPAN)
    causal = (row_ids[:, None] >= row_ids[None, :])[None]

    def advance(state_now, pieces):
        x_piece, step_piece, b_piece, c_piece = pieces
        cumulus = jnp.cumsum(step_piece * decay_rates[None, :], axis=0).T
        differ = cumulus[:, :, None] - cumulus[:, None, :]
        decay_mask = jnp.where(causal, jnp.exp(jnp.where(causal, differ, 0.0)), 0.0)
        scores = jnp.dot(c_piece, b_piece.T, precision=highest)
        weights = scores[None] * decay_mask * step_piece.T[:, None, :]
        inner_out = jnp.einsum("hij,jhp->ihp", weights, x_piece, precision=highest)
        carried = (
            jnp.einsum("in,hpn->ihp", c_piece, state_now, precision=highest)
            * jnp.exp(cumulus).T[:, :, None]
        )
        tail_weight = jnp.exp(cumulus[:, -1:] - cumulus) * step_piece.T
        fresh_state = jnp.einsum("hj,jhp,jn->hpn", tail_weight, x_piece, b_piece, precision=highest)
        new_state = state_now * jnp.exp(cumulus[:, -1])[:, None, None] + fresh_state
        return (new_state, inner_out + carried)

    zero_state = jnp.zeros((head_count, head_width, states), jnp.float32)
    last_state, block_outs = lax.scan(
        jax.checkpoint(advance), zero_state, (x_blocks, step_blocks, b_blocks, c_blocks)
    )
    return block_outs.reshape(length, head_count, head_width)


def mixer_heads(x_part, bc_part, dt_part, conv_w, conv_b, dt_shift, log_rate, skip_gain):
    length = x_part.shape[0]
    head_count = dt_part.shape[1]
    kernel = conv_w.shape[0]
    states = bc_part.shape[1] // 2
    inner_width = x_part.shape[1]
    joined = jnp.concatenate([x_part, bc_part], axis=1)
    padded = jnp.pad(joined, ((kernel - 1, 0), (0, 0)))
    conv_sum = conv_b[None, :] + sum(
        (conv_w[offset][None, :] * padded[offset : offset + length] for offset in range(kernel))
    )
    active = jax.nn.silu(conv_sum)
    x_conv = active[:, :inner_width].reshape(length, head_count, inner_width // head_count)
    b_conv = active[:, inner_width : inner_width + states]
    c_conv = active[:, inner_width + states :]
    step_size = jax.nn.softplus(dt_part + dt_shift[None, :])
    decay_rates = -jnp.exp(log_rate)
    mixed_out = (
        scan_blocks(x_conv, step_size, decay_rates, b_conv, c_conv)
        + skip_gain[None, :, None] * x_conv
    )
    return mixed_out.reshape(length, inner_width)


def gate_norm(mixed_values, gate_values, gain_values):
    return rms_scale(mixed_values * jax.nn.silu(gate_values), gain_values)


def contract_rows(left_side, right_side):
    return lax.dot_general(
        left_side, right_side, (((0,), (0,)), ((), ())), preferred_element_type=jnp.float32
    )


def contract_cols(left_side, right_side):
    return lax.dot_general(
        left_side, right_side, (((1,), (1,)), ((), ())), preferred_element_type=jnp.float32
    )


def body(
    hidden,
    out_grad,
    norm_gain,
    in_weight,
    conv_weight,
    conv_bias,
    dt_bias,
    a_log,
    d_skip,
    out_gain,
    out_weight,
):
    micro_count = hidden.shape[0]
    row_count = hidden.shape[1]
    model_width = hidden.shape[2]
    seq_count = lax.axis_size("seq")
    section_id = lax.axis_index("section")
    group_id = lax.axis_index("seq")
    gain_in = norm_gain[0]
    gain_out = out_gain[0]
    head_count = dt_bias.shape[1]
    heads_here = head_count // seq_count
    inner_width = out_gain.shape[1]
    proj_width = in_weight.shape[2]
    states = (proj_width - 2 * inner_width - head_count) // 2
    width_here = heads_here * HDIM
    x_start = group_id * width_here
    head_start = group_id * heads_here
    conv_full = conv_weight[0]
    kernel = conv_full.shape[0]
    conv_here = jnp.concatenate(
        [lax.dynamic_slice_in_dim(conv_full, x_start, width_here, 1), conv_full[:, inner_width:]],
        axis=1,
    )
    bias_here = jnp.concatenate(
        [
            lax.dynamic_slice_in_dim(conv_bias[0], x_start, width_here, 0),
            conv_bias[0][inner_width:],
        ],
        axis=0,
    )
    shift_here = lax.dynamic_slice_in_dim(dt_bias[0], head_start, heads_here, 0)
    rate_here = lax.dynamic_slice_in_dim(a_log[0], head_start, heads_here, 0)
    skip_here = lax.dynamic_slice_in_dim(d_skip[0], head_start, heads_here, 0)
    head_params = (conv_here, bias_here, shift_here, rate_here, skip_here)
    w_in_full, w_out_full = (
        lax.all_gather(in_weight[0], "wshard", axis=0, tiled=True),
        lax.all_gather(out_weight[0], "wshard", axis=0, tiled=True),
    )
    received = jnp.zeros((row_count, model_width), jnp.bfloat16)
    fwd_outs = []
    kept_list = []
    for tick_now in range(micro_count + 1):
        own_input = hidden[min(tick_now, micro_count - 1)]
        layer_input = jnp.where(section_id == 0, own_input, received)
        forward_inputs = layer_input.astype(jnp.float32)
        forward_normed = rms_scale(forward_inputs, gain_in).astype(jnp.bfloat16)
        projected = jnp.dot(forward_normed, w_in_full, preferred_element_type=jnp.float32)
        forward_gate_part = projected[:, :inner_width]
        x_send = projected[:, inner_width : 2 * inner_width].astype(jnp.bfloat16)
        bc_send = projected[:, 2 * inner_width : 2 * inner_width + 2 * states].astype(jnp.bfloat16)
        dt_send = projected[:, 2 * inner_width + 2 * states :].astype(jnp.bfloat16)
        forward_x_heads = lax.all_to_all(x_send, "seq", split_axis=1, concat_axis=0, tiled=True)
        forward_dt_heads = lax.all_to_all(dt_send, "seq", split_axis=1, concat_axis=0, tiled=True)
        forward_bc_whole = lax.all_gather(bc_send, "seq", axis=0, tiled=True)
        mixed_heads = mixer_heads(
            forward_x_heads.astype(jnp.float32),
            forward_bc_whole.astype(jnp.float32),
            forward_dt_heads.astype(jnp.float32),
            *head_params
        ).astype(jnp.bfloat16)
        forward_mixed_out = lax.all_to_all(
            mixed_heads, "seq", split_axis=0, concat_axis=1, tiled=True
        )
        forward_gated_out = gate_norm(
            forward_mixed_out.astype(jnp.float32), forward_gate_part, gain_out
        ).astype(jnp.bfloat16)
        branch = jnp.dot(forward_gated_out, w_out_full, preferred_element_type=jnp.float32)
        result = (forward_inputs + branch).astype(jnp.bfloat16)
        kept_values = (
            forward_gate_part,
            forward_mixed_out,
            forward_x_heads,
            forward_bc_whole,
            forward_dt_heads,
        )
        fwd_outs.append(result)
        kept_list.append((layer_input, kept_values))
        if tick_now < micro_count:
            received = from_behind(result, "section", 1)
    all_outs = jnp.stack(fwd_outs)
    layer_out = lax.dynamic_slice_in_dim(all_outs, section_id, micro_count, 0)[None]
    kept_all = jax.tree.map(lambda *members: jnp.stack(members), *kept_list)
    w_in_back, w_out_back = (
        lax.all_gather(in_weight[0], "wshard", axis=0, tiled=True),
        lax.all_gather(out_weight[0], "wshard", axis=0, tiled=True),
    )
    received_grad = jnp.zeros((row_count, model_width), jnp.bfloat16)
    grad_records = []
    product_rows = []
    small_totals = None
    for tick_now in range(micro_count + 1):
        micro_now = tick_now - 1 + section_id
        is_valid = (micro_now >= 0) & (micro_now < micro_count)
        own_grad = out_grad[min(tick_now, micro_count - 1)]
        grad_out = jnp.where(section_id == 1, own_grad, received_grad).astype(jnp.float32)
        grad_out = jnp.where(is_valid, grad_out, 0.0)
        slot_index = jnp.clip(tick_now - 1 + 2 * section_id, 0, micro_count)
        input_values, kept_values = jax.tree.map(
            lambda member: lax.dynamic_index_in_dim(member, slot_index, 0, keepdims=False), kept_all
        )
        gate_part, mixed_out, x_heads, bc_whole, dt_heads = kept_values
        inputs = input_values.astype(jnp.float32)
        gated_f, gate_pull = jax.vjp(gate_norm, mixed_out.astype(jnp.float32), gate_part, gain_out)
        gated_out = gated_f.astype(jnp.bfloat16)
        grad_branch = grad_out.astype(jnp.bfloat16)
        grad_gated = contract_cols(grad_branch, w_out_back)
        grad_mixed, grad_gate, backward_grad_gain_out = gate_pull(grad_gated)
        grad_mixed_heads = lax.all_to_all(
            grad_mixed.astype(jnp.bfloat16), "seq", split_axis=1, concat_axis=0, tiled=True
        )
        mixed_again, head_pull = jax.vjp(
            mixer_heads,
            x_heads.astype(jnp.float32),
            bc_whole.astype(jnp.float32),
            dt_heads.astype(jnp.float32),
            *head_params
        )
        (
            grad_x,
            grad_bc,
            grad_dt,
            backward_grad_conv,
            backward_grad_bias,
            backward_grad_shift,
            backward_grad_rate,
            backward_grad_skip,
        ) = head_pull(grad_mixed_heads.astype(jnp.float32))
        grad_x_tok = lax.all_to_all(
            grad_x.astype(jnp.bfloat16), "seq", split_axis=0, concat_axis=1, tiled=True
        )
        grad_dt_tok = lax.all_to_all(
            grad_dt.astype(jnp.bfloat16), "seq", split_axis=0, concat_axis=1, tiled=True
        )
        grad_bc_tok = lax.psum_scatter(
            grad_bc.astype(jnp.bfloat16), "seq", scatter_dimension=0, tiled=True
        ).astype(jnp.float32)
        grad_proj = jnp.concatenate(
            [
                grad_gate,
                grad_x_tok.astype(jnp.float32),
                grad_bc_tok,
                grad_dt_tok.astype(jnp.float32),
            ],
            axis=1,
        ).astype(jnp.bfloat16)
        normed_f, norm_pull = jax.vjp(rms_scale, inputs, gain_in)
        normed = normed_f.astype(jnp.bfloat16)
        grad_normed = contract_cols(grad_proj, w_in_back)
        grad_inputs, backward_grad_gain_in = norm_pull(grad_normed)
        small_terms = (
            backward_grad_gain_in,
            backward_grad_conv,
            backward_grad_bias,
            backward_grad_shift,
            backward_grad_rate,
            backward_grad_skip,
            backward_grad_gain_out,
        )
        grad_total, small_terms, product_terms = (
            grad_out + grad_inputs,
            small_terms,
            (normed, grad_proj, gated_out, grad_branch),
        )
        small_totals = (
            small_terms
            if small_totals is None
            else jax.tree.map(jnp.add, small_totals, small_terms)
        )
        product_rows.append(product_terms)
        sent_grad = grad_total.astype(jnp.bfloat16)
        grad_records.append(jnp.where(section_id == 1, sent_grad.astype(jnp.float32), grad_total))
        if tick_now < micro_count:
            received_grad = from_behind(sent_grad, "section", -1)
    all_grads = jnp.stack(grad_records)
    section_grad = lax.dynamic_slice_in_dim(all_grads, 1 - section_id, micro_count, 0)[None]
    normed_all = jnp.concatenate([terms[0] for terms in product_rows], axis=0)
    grad_proj_all = jnp.concatenate([terms[1] for terms in product_rows], axis=0)
    gated_all = jnp.concatenate([terms[2] for terms in product_rows], axis=0)
    branch_all = jnp.concatenate([terms[3] for terms in product_rows], axis=0)
    grad_w_in = contract_rows(normed_all, grad_proj_all)
    grad_w_out = contract_rows(gated_all, branch_all)
    owned_grads = (
        lax.psum_scatter(
            grad_w_in.astype(jnp.bfloat16), "wshard", scatter_dimension=0, tiled=True
        ).astype(jnp.float32),
        lax.psum_scatter(
            grad_w_out.astype(jnp.bfloat16), "wshard", scatter_dimension=0, tiled=True
        ).astype(jnp.float32),
    )
    owned_grads = (
        lax.psum(owned_grads[0].astype(jnp.bfloat16), "seq").astype(jnp.float32),
        lax.psum(owned_grads[1].astype(jnp.bfloat16), "seq").astype(jnp.float32),
    )
    grad_gain_in, grad_conv, grad_bias, grad_shift, grad_rate, grad_skip, grad_gain_out = (
        small_totals
    )
    conv_x_full = lax.dynamic_update_slice_in_dim(
        jnp.zeros((kernel, inner_width), jnp.float32), grad_conv[:, :width_here], x_start, 1
    )
    conv_grad_full = jnp.concatenate([conv_x_full, grad_conv[:, width_here:]], axis=1)
    bias_x_full = lax.dynamic_update_slice_in_dim(
        jnp.zeros((inner_width,), jnp.float32), grad_bias[:width_here], x_start, 0
    )
    bias_grad_full = jnp.concatenate([bias_x_full, grad_bias[width_here:]], axis=0)
    head_zeros = jnp.zeros((head_count,), jnp.float32)
    shift_full = lax.dynamic_update_slice_in_dim(head_zeros, grad_shift, head_start, 0)
    rate_full = lax.dynamic_update_slice_in_dim(head_zeros, grad_rate, head_start, 0)
    skip_full = lax.dynamic_update_slice_in_dim(head_zeros, grad_skip, head_start, 0)
    small_grads = lax.psum(
        (
            grad_gain_in,
            conv_grad_full,
            bias_grad_full,
            shift_full,
            rate_full,
            skip_full,
            grad_gain_out,
        ),
        ("seq", "wshard"),
    )
    return (
        layer_out,
        section_grad,
        small_grads[0][None],
        owned_grads[0][None],
        small_grads[1][None],
        small_grads[2][None],
        small_grads[3][None],
        small_grads[4][None],
        small_grads[5][None],
        small_grads[6][None],
        owned_grads[1][None],
    )


def solution(mesh):
    in_specs = (
        P("wshard", "seq", None),
        P("wshard", "seq", None),
        P("section", None),
        P("section", "wshard", None),
        P("section", None, None),
        P("section", None),
        P("section", None),
        P("section", None),
        P("section", None),
        P("section", None),
        P("section", "wshard", None),
    )
    out_specs = (
        P("section", "wshard", "seq", None),
        P("section", "wshard", "seq", None),
        P("section", None),
        P("section", "wshard", None),
        P("section", None, None),
        P("section", None),
        P("section", None),
        P("section", None),
        P("section", None),
        P("section", None),
        P("section", "wshard", None),
    )
    return jax.shard_map(body, mesh=mesh, in_specs=in_specs, out_specs=out_specs, check_vma=False)
```

profile of v0, /device:TPU:0, one launch (start us, length us, event | category | flops | bytes accessed | tf_op | source)
XLA Modules:
  0.0 2160.4 jit_solution(13809559952216919172)
XLA Ops:
  9.1 95.5 %all-gather.14.cloned.1.call-done = bf16[1,1024,4384]{1,2,0:T(8,128)(2,1)} async-done(((bf16[1,256,4384]{1,2,0:T(8,128)(2,1)}), bf16[1,1024,4384]{1,2,0:T(8,128)(2,1)}) %all-gather.14.cloned.1.call-update) | async-done | bytes 8978448 | tf_op jit(solution)/shard_map/all_gather | solution.py:146
  134.7 8.3 all-to-all-done.1
  143.1 15.2 all-gather.8.cloned.1.call-done
  172.2 92.1 %while.162 = (s32[]{:T(128)}, f32[2,64,128]{2,1,0:T(8,128)S(1)}, f32[8,256,2,64]{1,0,3,2:T(8,128)}, f32[8,256,2]{1,0,2:T(8,128)S(1)}, f32[2]{0:T(128)S(1)}, /*in...) while((s32[]{:T(128)}, f32[2,64,128]{2,1,0:T(8,128)S(1)}, ...), condition=%wide.region_4.5_spmd.clone.clone, body=%wide.region_1.4_spmd.clone.clone.sunk | while | flops 302941696 | bytes 2864444 | solution.py:53
  266.1 14.7 all_to_all.261
  290.3 7.6 fusion.545
  314.4 10.4 all-to-all-done.4
  325.0 17.5 all-gather.10.cloned.1.call-done
  356.2 92.0 %while.163 = (s32[]{:T(128)}, f32[2,64,128]{2,1,0:T(8,128)S(1)}, f32[8,256,2,64]{1,0,3,2:T(8,128)}, f32[8,256,2]{1,0,2:T(8,128)S(1)}, f32[2]{0:T(128)S(1)}, /*in...) while((s32[]{:T(128)}, f32[2,64,128]{2,1,0:T(8,128)S(1)}, ...), condition=%wide.region_10.11_spmd.clone.clone, body=%wide.region_7.10_spmd.clone.clone.sunk | while | flops 302941696 | bytes 2864444 | solution.py:53
  450.1 15.1 all_to_all.262
  469.8 11.5 collective-permute-start.1
  481.5 7.6 fusion.546
  508.3 8.3 all-to-all-done.7
  521.6 13.5 all-gather.12.cloned.1.call-done
  544.3 25.1 %fusion.323 = (f32[2048,384]{0,1:T(8,128)}, f32[2048,384]{0,1:T(8,128)}, f32[2048,384]{0,1:T(8,128)}, f32[2048,384]{0,1:T(8,128)}, f32[2048,384]{0,1:T(8,128)}, /*index=5*/f32[2048,384]{0,1:T(8,128)}, f32[2048,384]{0,1:T(8,128)}) fusion(f32[2048,384]{0,1:T(8,128)S(1)} %maximum_convert_fusion.5, f32[384]{0:T(512)S(1)} %get-tuple-element.2181, ...), kind=kLoop, calls=%fused_computation.520 | loop fusion | flops 37748736 | bytes 34610688 | tf_op jit(solution)/shard_map/jvp(jit(silu))/mul | solution.py:70
  576.7 69.9 %while.164 = (s32[]{:T(128)}, f32[2,64,128]{2,1,0:T(8,128)S(1)}, f32[8,256,2,64]{1,0,3,2:T(8,128)}, f32[8,256,2]{1,0,2:T(8,128)S(1)}, f32[2]{0:T(128)S(1)}, /*in...) while((s32[]{:T(128)}, f32[2,64,128]{2,1,0:T(8,128)S(1)}, ...), condition=%wide.region_16.17_spmd.clone.clone, body=%wide.region_13.16_spmd.clone.clone.sunk | while | flops 302941696 | bytes 2996020 | solution.py:53
  657.4 8.8 all-to-all-done.8
  700.5 31.7 %while.156 = (s32[]{:T(128)}, f32[2,64,128]{2,1,0:T(8,128)S(1)}, f32[8,2,64,128]{3,2,1,0:T(8,128)S(1)}, f32[8,256,2]{1,2,0:T(2,128)}, f32[1,2]{1,0:T(1,128)S(1)}...) while((s32[]{:T(128)}, f32[2,64,128]{2,1,0:T(8,128)S(1)}, ...), condition=%wide.region_23.25_spmd.clone, body=%wide.region_20.24_spmd.clone.sunk | while | flops 50497032 | bytes 555299 | solution.py:53
  742.0 147.0 %while.157 = (s32[]{:T(128)}, f32[2]{0:T(128)S(1)}, f32[2,64,128]{2,1,0:T(8,128)S(1)}, f32[8,256,2,64]{1,0,3,2:T(8,128)}, f32[8,256,2]{1,2,0:T(2,128)S(1)}, /*in...) while((s32[]{:T(128)}, f32[2]{0:T(128)S(1)}, ...), condition=%wide.region_37.39_spmd.clone, body=%wide.region_24.38_spmd.clone.sunk | while | flops 758179328 | bytes 7640696 | solution.py:53
  932.3 55.1 %reduce-scatter.16.cloned.1.call-done = bf16[128,256]{1,0:T(8,128)(2,1)} async-done(((bf16[2048,256]{1,0:T(8,128)(2,1)}), bf16[128,256]{1,0:T(8,128)(2,1)}) %reduce-scatter.16.cloned.1.call-update) | async-done | bytes 65552
  1013.2 11.8 all-to-all-done.12
  1031.9 31.9 %while.158 = (s32[]{:T(128)}, f32[2,64,128]{2,1,0:T(8,128)S(1)}, f32[8,2,64,128]{3,2,1,0:T(8,128)S(1)}, f32[8,256,2]{1,2,0:T(2,128)}, f32[1,2]{1,0:T(1,128)S(1)}...) while((s32[]{:T(128)}, f32[2,64,128]{2,1,0:T(8,128)S(1)}, ...), condition=%wide.region_46.48_spmd.clone, body=%wide.region_43.47_spmd.clone.sunk | while | flops 50497032 | bytes 555299 | solution.py:53
  1073.6 146.9 %while.159 = (s32[]{:T(128)}, f32[2]{0:T(128)S(1)}, f32[2,64,128]{2,1,0:T(8,128)S(1)}, f32[8,256,2,64]{1,0,3,2:T(8,128)}, f32[8,256,2]{1,2,0:T(2,128)S(1)}, /*in...) while((s32[]{:T(128)}, f32[2]{0:T(128)S(1)}, ...), condition=%wide.region_60.62_spmd.clone, body=%wide.region_47.61_spmd.clone.sunk | while | flops 758179328 | bytes 7640696 | solution.py:53
  1262.2 57.0 %reduce-scatter.18.cloned.1.call-done = bf16[128,256]{1,0:T(8,128)(2,1)} async-done(((bf16[2048,256]{1,0:T(8,128)(2,1)}), bf16[128,256]{1,0:T(8,128)(2,1)}) %reduce-scatter.18.cloned.1.call-update) | async-done | bytes 65552
  1346.6 11.8 all-to-all-done.15
  1365.3 31.9 %while.160 = (s32[]{:T(128)}, f32[2,64,128]{2,1,0:T(8,128)S(1)}, f32[8,2,64,128]{3,2,1,0:T(8,128)S(1)}, f32[8,256,2]{1,2,0:T(2,128)}, f32[1,2]{1,0:T(1,128)S(1)}...) while((s32[]{:T(128)}, f32[2,64,128]{2,1,0:T(8,128)S(1)}, ...), condition=%wide.region_69.71_spmd.clone, body=%wide.region_66.70_spmd.clone.sunk | while | flops 50497032 | bytes 555299 | solution.py:53
  1407.0 147.0 %while.161 = (s32[]{:T(128)}, f32[2]{0:T(128)S(1)}, f32[2,64,128]{2,1,0:T(8,128)S(1)}, f32[8,256,2,64]{1,0,3,2:T(8,128)}, f32[8,256,2]{1,2,0:T(2,128)S(1)}, /*in...) while((s32[]{:T(128)}, f32[2]{0:T(128)S(1)}, ...), condition=%wide.region_83.85_spmd.clone, body=%wide.region_70.84_spmd.clone.sunk | while | flops 758179328 | bytes 7640696 | solution.py:53
  1602.6 49.8 %reduce-scatter.20.cloned.1.call-done = bf16[128,256]{1,0:T(8,128)(2,1)} async-done(((bf16[2048,256]{1,0:T(8,128)(2,1)}), bf16[128,256]{1,0:T(8,128)(2,1)}) %reduce-scatter.20.cloned.1.call-update) | async-done | bytes 65552
  1659.7 15.5 convolution_convert_fusion
  1675.9 25.7 %reduce-scatter.14.cloned.1.call-done = bf16[512,1024]{1,0:T(8,128)(2,1)} async-done(((bf16[2048,1024]{1,0:T(8,128)(2,1)}), bf16[512,1024]{1,0:T(8,128)(2,1)}) %reduce-scatter.14.cloned.1.call-update) | async-done | bytes 1048592 | tf_op jit(solution)/shard_map/reduce_scatter | solution.py:296
  1701.6 87.3 %reduce-scatter.12.cloned.1.call-done = bf16[256,4384]{0,1:T(8,128)(2,1)} async-done(((bf16[1024,4384]{0,1:T(8,128)(2,1)}), bf16[256,4384]{0,1:T(8,128)(2,1)}) %reduce-scatter.12.cloned.1.call-update) | async-done | bytes 2244624 | tf_op jit(solution)/shard_map/reduce_scatter | solution.py:293
  1796.9 347.8 %all-reduce.45 = (f32[1,1024]{1,0:T(1,128)}, f32[1,4,2304]{2,1,0:T(4,128)}, f32[1,2304]{1,0:T(1,128)}, f32[1,32]{1,0:T(1,128)}, f32[1,32]{1,0:T(1,128)}, /*index=5*/f32[1,32]{1,0:T(1,128)}, f32[1,2048]{1,0:T(1,128)}) all-reduce(f32[1,1024]{1,0:T(1,128)S(1)} %bitcast.1888, ...), channel_id=1, replica_groups=mesh['section'=2,'seq'=16,'wshard'=4] {'seq','wshard'}, use_global_device_ids=true, to_apply=%region_90.92 | all-reduce | flops 14688 | bytes 117504 | tf_op jit(solution)/shard_map/psum | solution.py:319
  (2516 shorter events, 1216.8 us)
Async XLA Ops:
  7.2 97.4 %all-gather.14.cloned.1.call-start = ((), (), s32[]{:S(2)}) async-start(), calls=%async_computation.28 | async-start | bytes 11223040 | tf_op jit(solution)/shard_map/all_gather | solution.py:146
  7.9 150.4 %all-gather.8.cloned.1.call-start = ((), (), s32[]{:S(2)}) async-start(), calls=%async_computation.23 | async-start | bytes 1114112 | tf_op jit(solution)/shard_map/all_gather | solution.py:164
  112.8 171.3 %all-gather.16.cloned.1.call-start = ((), (), s32[]{:S(2)}) async-start(), calls=%async_computation.29 | async-start | bytes 5242880 | tf_op jit(solution)/shard_map/all_gather | solution.py:147
  114.9 14.5 all-to-all-start
  129.4 13.7 all-to-all-start.1
  132.9 209.5 %all-gather.10.cloned.1.call-start = ((), (), s32[]{:S(2)}) async-start(), calls=%async_computation.24 | async-start | bytes 1114112 | tf_op jit(solution)/shard_map/all_gather | solution.py:164
  134.0 410.3 %copy-start.98 = (f32[384]{0:T(512)}, f32[384]{0:T(512)S(1)}, u32[]{:S(2)}) copy-start(f32[384]{0:T(512)S(1)} %get-tuple-element.2179) | copy-start | bytes 4612
  287.6 2.4 collective-permute-start
  299.1 10.9 all-to-all-start.3
  310.1 14.7 all-to-all-start.4
  313.6 221.4 %all-gather.12.cloned.1.call-start = ((), (), s32[]{:S(2)}) async-start(), calls=%async_computation.25 | async-start | bytes 1114112 | tf_op jit(solution)/shard_map/all_gather | solution.py:164
  469.8 11.5 collective-permute-start.1
  492.0 10.9 all-to-all-start.6
  502.9 13.7 all-to-all-start.7
  650.8 15.4 all-to-all-start.8
  678.8 14.7 all-to-all-start.9
  683.3 304.2 %reduce-scatter.16.cloned.1.call-start = ((), (), s32[]{:S(2)}) async-start(), calls=%async_computation.30 | async-start | bytes 1114112
  916.5 10.9 all-to-all-start.11
  927.4 61.0 %all-to-all-start.10 = ((bf16[16,128,128]{1,2,0:T(8,128)(2,1)}), bf16[16,128,128]{1,2,0:T(8,128)(2,1)S(1)}, u32[]{:S(2)}, u32[]{:S(2)}) async-start(bf16[16,128,128]{1,2,0:T(8,128)(2,1)} %copy_bitcast_fusion.28), calls=%async_computation.10 | async-start | bytes 1048576 | tf_op jit(solution)/shard_map/all_to_all | solution.py:238
  996.3 3.4 collective-permute-start.2
  1008.1 16.9 all-to-all-start.12
  1013.1 306.1 %reduce-scatter.18.cloned.1.call-start = ((), (), s32[]{:S(2)}) async-start(), calls=%async_computation.31 | async-start | bytes 1114112
  1247.7 10.9 all-to-all-start.14
  1258.6 61.6 %all-to-all-start.13 = ((bf16[16,128,128]{1,2,0:T(8,128)(2,1)}), bf16[16,128,128]{1,2,0:T(8,128)(2,1)S(1)}, u32[]{:S(2)}, u32[]{:S(2)}) async-start(bf16[16,128,128]{1,2,0:T(8,128)(2,1)} %copy_bitcast_fusion.27), calls=%async_computation.13 | async-start | bytes 1048576 | tf_op jit(solution)/shard_map/all_to_all | solution.py:238
  1329.7 3.4 collective-permute-start.3
  1341.5 16.8 all-to-all-start.15
  1346.5 306.0 %reduce-scatter.20.cloned.1.call-start = ((), (), s32[]{:S(2)}) async-start(), calls=%async_computation.32 | async-start | bytes 1114112
  1579.3 122.2 %reduce-scatter.14.cloned.1.call-start = ((), (), s32[]{:S(2)}) async-start(), calls=%async_computation.27 | async-start | bytes 5242880 | tf_op jit(solution)/shard_map/reduce_scatter | solution.py:296
  1588.1 10.9 all-to-all-start.17
  1599.0 54.4 %all-to-all-start.16 = ((bf16[16,128,128]{1,2,0:T(8,128)(2,1)}), bf16[16,128,128]{1,2,0:T(8,128)(2,1)S(1)}, u32[]{:S(2)}, u32[]{:S(2)}) async-start(bf16[16,128,128]{1,2,0:T(8,128)(2,1)} %copy_bitcast_fusion.26), calls=%async_computation.16 | async-start | bytes 1048576 | tf_op jit(solution)/shard_map/all_to_all | solution.py:238
  1602.6 186.4 %reduce-scatter.12.cloned.1.call-start = ((), (), s32[]{:S(2)}) async-start(), calls=%async_computation.26 | async-start | bytes 11223040 | tf_op jit(solution)/shard_map/reduce_scatter | solution.py:293
  1675.2 472.4 %all-reduce.49.cloned.1.call-start = ((), (), s32[]{:S(2)}) async-start(), calls=%async_computation.33 | async-start | bytes 6586368 | tf_op jit(solution)/shard_map/psum | solution.py:301
  (186 other events, 5725.7 us)
Sparse Core Ops, SparseCore 0:
  9.7 94.8 all-gather.13
  112.9 45.3 all-gather.7
  160.0 47.4 all-gather.15
  298.7 43.7 all-gather.9
  490.9 44.1 all-gather.11
  914.6 72.8 reduce-scatter.15
  1246.4 72.8 reduce-scatter.17
  1579.5 72.9 reduce-scatter.19
  1655.6 45.9 reduce-scatter.13
  1703.9 84.9 reduce-scatter.11
  1792.5 97.1 all-reduce.48
where the time goes:
time: 2180 us; the launch traced here: 2160 us
  waiting for transfers between devices  520 us (24%)
  local copies, waits for them, and re-layouts  474 us (22%)
  blocking collectives  378 us (17%)
  other arithmetic  343 us (16%)
  matrix products  341 us (16%)
  starting transfers between devices  81.8 us (4%)
    psum x1, blocking collectives, body(): lax.psum((grad_gain_in, conv_grad_full, bias_grad_full, shift_full, rate_...  348 us
    dynamic_update_slice x96, local copies, waits for them, and re-layouts, scan_blocks(): lax.scan(jax.checkpoint(advance), zero_state, (x_blocks, step_blocks, b_b...  202 us
    unnamed x14, waiting for transfers between devices  164 us
    another operation x261, other arithmetic  158 us
    all_gather x1, waiting for transfers between devices, body(): lax.all_gather(in_weight[0], 'wshard', axis=0, tiled=True)  95.5 us
    dot_general x96, matrix products, advance(): scores = jnp.dot(c_piece, b_piece.T, precision=highest)  88.9 us
    reduce_scatter x1, waiting for transfers between devices, body(): lax.psum_scatter(grad_w_in.astype(jnp.bfloat16), 'wshard', scatter_dimens...  87.3 us
    unnamed x407, local copies, waits for them, and re-layouts  71.8 us
  transfers between devices with their start and end apart: 31, of which 25 were waited for; matrix products, arithmetic and copies ran while one was open for 9% of the time, Pallas kernels for 0%

commit v1 on v0

v1 whole, which is shorter than its diff:
```python
import functools

import jax
import jax.numpy as jnp
from jax import lax
from jax.experimental import pallas as pl
from jax.experimental.pallas import tpu as pltpu
from jax.sharding import PartitionSpec as P

F32 = jnp.float32
BF16 = jnp.bfloat16
HI = lax.Precision.HIGHEST
EPS = 1e-05
HDIM = 64
LANE = 128
TAIL = 16


def shift(x, axis, by):
    devices = lax.axis_size(axis)
    pairs = [(i, i + by) for i in range(devices) if 0 <= i + by < devices]
    return lax.ppermute(x, axis, pairs)


def swap(x):
    return lax.ppermute(x, "section", [(0, 1), (1, 0)])


def half(a, which):
    width = a.shape[-1] // 8
    b = a.reshape(a.shape[:-1] + (4, 2, width))
    b = lax.dynamic_index_in_dim(b, which, axis=b.ndim - 2, keepdims=False)
    return b.reshape(a.shape[:-1] + (4 * width,))


def whole(own, other, core):
    width = own.shape[-1] // 4
    lead = own.shape[:-1]
    own, other = own.reshape(lead + (4, 1, width)), other.reshape(lead + (4, 1, width))
    first, second = jnp.where(core == 0, own, other), jnp.where(core == 0, other, own)
    return jnp.concatenate([first, second], axis=-2).reshape(lead + (8 * width,))


def mm(a, b):
    return jnp.dot(a.astype(BF16), b.astype(BF16), preferred_element_type=F32)


def mm_nt(a, b):
    return lax.dot_general(
        a.astype(BF16), b.astype(BF16), (((1,), (1,)), ((), ())), preferred_element_type=F32
    )


def mm_tn(a, b):
    return lax.dot_general(
        a.astype(BF16), b.astype(BF16), (((0,), (0,)), ((), ())), preferred_element_type=F32
    )


def spread_matrix(width):
    head = lax.broadcasted_iota(jnp.int32, (LANE, width), 0)
    lane = lax.broadcasted_iota(jnp.int32, (LANE, width), 1)
    return jnp.where(lane // HDIM == head, 1.0, 0.0).astype(F32)


def spread(heads, matrix):
    return jnp.dot(heads, matrix, precision=HI, preferred_element_type=F32)


def gather_heads(lanes, matrix):
    return lax.dot_general(
        lanes, matrix, (((1,), (1,)), ((), ())), precision=HI, preferred_element_type=F32
    )


def tri(rows, upper):
    r = lax.broadcasted_iota(jnp.int32, (rows, rows), 0)
    c = lax.broadcasted_iota(jnp.int32, (rows, rows), 1)
    return jnp.where((c >= r) if upper else (r >= c), 1.0, 0.0).astype(F32)


def steps(dt, hp):
    shifted = dt + hp[0:1, :]
    step = jnp.maximum(shifted, 0.0) + jnp.log1p(jnp.exp(-jnp.abs(shifted)))
    rate = -jnp.exp(hp[1:2, :])
    return shifted, step, rate


def sigmoid(v):
    return 1.0 / (1.0 + jnp.exp(-v))


def conv_pre(buf, cw, cb, taps, rows):
    pre = cb[0:1, :]
    for k in range(taps):
        start = TAIL - (taps - 1) + k
        pre = pre + cw[k : k + 1, :] * buf[start : start + rows, :]
    return pre


def chunk_kernel(taps, xbc, halo, dt, cw, cb, hp, act_o, cum_o, step_o, sloc_o, buf):
    rows, inner = xbc.shape[1], sloc_o.shape[0] * LANE
    buf[0:TAIL, :] = halo[0].astype(F32)
    buf[TAIL : TAIL + rows, :] = xbc[0].astype(F32)
    pre = conv_pre(buf, cw, cb, taps, rows)
    act = pre * sigmoid(pre)
    act_o[0] = act
    _, step, rate = steps(dt[0].astype(F32), hp)
    cum = jnp.dot(tri(rows, False), step * rate, precision=HI, preferred_element_type=F32)
    cum_o[0] = cum
    step_o[0] = step
    last = cum[rows - 1 : rows, :]
    matrix = spread_matrix(inner)
    weight = spread(jnp.exp(last - cum) * step, matrix)
    decay = spread(jnp.broadcast_to(jnp.exp(last), (8, LANE)), matrix)[0:1, :]
    d_hi = decay.astype(BF16).astype(F32)
    d_mid = (decay - d_hi).astype(BF16).astype(F32)
    d_lo = decay - d_hi - d_mid
    row = lax.broadcasted_iota(jnp.int32, (TAIL, inner), 0)
    extra = jnp.where(row == 0, d_hi, jnp.where(row == 1, d_mid, jnp.where(row == 2, d_lo, 0.0)))
    extra = extra.astype(BF16)
    xw = (act[:, :inner] * weight).astype(BF16)
    b = act[:, inner : inner + LANE].astype(BF16)
    sloc = mm_tn(b, xw).astype(BF16)
    states = sloc.shape[0]
    for i in range(inner // LANE):
        sloc_o[i, 0:states, :] = sloc[:, i * LANE : (i + 1) * LANE]
        sloc_o[i, states : states + TAIL, :] = extra[:, i * LANE : (i + 1) * LANE]


def prefix_kernel(reverse, with_decay, r, *refs):
    pieces, states = r.shape[0], refs[-1].shape[1]
    if with_decay:
        decay_o, out = refs
        for j in range(pieces):
            tail = r[j, states : states + TAIL, :].astype(F32)
            decay_o[j : j + 1, :] = tail[0:1, :] + tail[1:2, :] + tail[2:3, :]
        decay = decay_o
    else:
        decay, out = refs
    carry = jnp.zeros((states, LANE), F32)
    order = range(pieces - 1, -1, -1) if reverse else range(pieces)
    for j in order:
        out[j] = carry.astype(BF16)
        carry = carry * decay[j : j + 1, :] + r[j, 0:states, :].astype(F32)


def intra_kernel(act, cum, step, yi_o):
    rows, inner = yi_o.shape[1], yi_o.shape[2]
    b = act[0, :, inner : inner + LANE]
    c = act[0, :, inner + LANE : inner + 2 * LANE]
    cb = mm_nt(c, b)
    cum_v = cum[0]
    cum_t = jnp.transpose(cum_v)
    xs = act[0, :, :inner] * spread(step[0], spread_matrix(inner))
    keep = tri(rows, False) > 0
    low = lax.broadcasted_iota(jnp.int32, (rows, LANE), 1) < HDIM
    for i in range(inner // LANE):
        xs_i = xs[:, i * LANE : (i + 1) * LANE].astype(BF16)
        parts = []
        for h in (2 * i, 2 * i + 1):
            diff = cum_v[:, h : h + 1] - cum_t[h : h + 1, :]
            decay = jnp.exp(jnp.where(keep, diff, -1e30))
            parts.append(mm(cb * decay, xs_i))
        yi_o[0, :, i * LANE : (i + 1) * LANE] = jnp.where(low, parts[0], parts[1])


def finish_kernel(act, cum, yi, sin, z, hp, gain, yy_o, gg_o, ss_o):
    inner = yi.shape[2]
    matrix = spread_matrix(inner)
    grown = spread(jnp.exp(cum[0]), matrix)
    skip = spread(jnp.broadcast_to(hp[2:3, :], (8, LANE)), matrix)[0:1, :]
    c = act[0, :, inner + LANE : inner + 2 * LANE].astype(BF16)
    total = jnp.zeros((yi.shape[1], LANE), F32)
    for i in range(inner // LANE):
        at = slice(i * LANE, (i + 1) * LANE)
        yy = yi[0, :, at] + grown[:, at] * mm(c, sin[i])
        yy_o[0, :, at] = yy
        mixed = (yy + skip[:, at] * act[0, :, at]).astype(BF16).astype(F32)
        zi = z[0, :, at]
        g = mixed * (zi * sigmoid(zi))
        total = total + g * g
        gg_o[0, :, at] = (g * gain[0:1, at]).astype(BF16)
    ss_o[0] = jnp.sum(total, axis=1, keepdims=True)


def gate_back_kernel(
    gr, z, yy, act, cum, rn, rs, hp, gain, dy_o, gz_o, dsl_o, dgain_o, gated_o
):
    inner = gr.shape[2]
    matrix = spread_matrix(inner)
    grown = spread(jnp.exp(cum[0]), matrix)
    skip = spread(jnp.broadcast_to(hp[2:3, :], (8, LANE)), matrix)[0:1, :]
    c = act[0, :, inner + LANE : inner + 2 * LANE].astype(BF16)
    r = rn[0]
    k = r * r * r * rs[0] * (1.0 / (2 * inner))
    for i in range(inner // LANE):
        at = slice(i * LANE, (i + 1) * LANE)
        mixed = (yy[0, :, at] + skip[:, at] * act[0, :, at]).astype(BF16).astype(F32)
        zi = z[0, :, at]
        sg = sigmoid(zi)
        silu = zi * sg
        g = mixed * silu
        gr_i = gr[0, :, at]
        gain_i = gain[0:1, at]
        normal = g * r
        dgain_o[0, :, at] = jnp.broadcast_to(
            jnp.sum(gr_i * normal, axis=0, keepdims=True), (8, LANE)
        )
        gated_o[0, :, at] = (normal * gain_i).astype(BF16)
        dg = r * (gain_i * gr_i) - g * k
        dy = (dg * silu).astype(BF16)
        dy_o[0, :, at] = dy
        gz_o[0, :, at] = (dg * mixed * (sg * (1.0 + zi * (1.0 - sg)))).astype(BF16)
        dsl_o[i] = mm_tn(c, dy.astype(F32) * grown[:, at]).astype(BF16)


def intra_back_kernel(act, cum, step, dy, dxs_o, dbc_o, dcum_o):
    rows, inner = dxs_o.shape[1], dxs_o.shape[2]
    b = act[0, :, inner : inner + LANE].astype(BF16)
    c = act[0, :, inner + LANE : inner + 2 * LANE].astype(BF16)
    cb = mm_nt(c, b)
    cum_v = cum[0]
    cum_t = jnp.transpose(cum_v)
    xs = act[0, :, :inner] * spread(step[0], spread_matrix(inner))
    keep = tri(rows, False) > 0
    low = lax.broadcasted_iota(jnp.int32, (rows, LANE), 1) < HDIM
    dcb = jnp.zeros((rows, rows), F32)
    lane = lax.broadcasted_iota(jnp.int32, (rows, LANE), 1)
    row_sums = jnp.zeros((rows, LANE), F32)
    col_sums = []
    for i in range(inner // LANE):
        at = slice(i * LANE, (i + 1) * LANE)
        xs_i = xs[:, at]
        dy_i = dy[0, :, at].astype(F32)
        parts = []
        for n, h in enumerate((2 * i, 2 * i + 1)):
            diff = cum_v[:, h : h + 1] - cum_t[h : h + 1, :]
            decay = jnp.exp(jnp.where(keep, diff, -1e30))
            mine = jnp.where(low, dy_i, 0.0) if n == 0 else jnp.where(low, 0.0, dy_i)
            flow = mm_nt(mine, xs_i) * decay
            dcb = dcb + flow
            both = flow * cb
            row_sums = jnp.where(lane == h, jnp.sum(both, axis=1, keepdims=True), row_sums)
            col_sums.append(jnp.sum(both, axis=0, keepdims=True))
            parts.append(mm_tn(cb * decay, dy_i))
        dxs_o[0, :, at] = jnp.where(low, parts[0], parts[1])
    col_sums.append(jnp.zeros((LANE - len(col_sums), rows), F32))
    dcum_o[0] = row_sums - jnp.transpose(jnp.concatenate(col_sums, axis=0))
    dbc_o[0, :, 0:LANE] = mm_tn(dcb, c)
    dbc_o[0, :, LANE : 2 * LANE] = mm(dcb, b)


def mix_back_kernel(
    taps, xbc, halo, dt, cw, cb, hp, act, cum, step, dy, dxs, dbc, dci, grad, sin,
    dpre_o, ddt_o, conv_o, head_o, buf, dact,
):
    rows, inner = dy.shape[1], dy.shape[2]
    matrix = spread_matrix(inner)
    cum_v, step_v = cum[0], step[0]
    last = cum_v[rows - 1 : rows, :]
    step_e = spread(step_v, matrix)
    tail_e = spread(jnp.exp(last - cum_v), matrix)
    grown = spread(jnp.exp(cum_v), matrix)
    d_e = grown[rows - 1 : rows, :]
    skip = spread(jnp.broadcast_to(hp[2:3, :], (8, LANE)), matrix)[0:1, :]
    b = act[0, :, inner : inner + LANE].astype(BF16)
    c = act[0, :, inner + LANE : inner + 2 * LANE].astype(BF16)
    q1 = dci[0]
    qb = jnp.zeros((rows, LANE), F32)
    q2 = jnp.zeros((rows, LANE), F32)
    flows = jnp.zeros((8, LANE), F32)
    skips = jnp.zeros((8, LANE), F32)
    db, dc = dbc[0, :, 0:LANE], dbc[0, :, LANE : 2 * LANE]
    for i in range(inner // LANE):
        at = slice(i * LANE, (i + 1) * LANE)
        g = grad[i]
        x = act[0, :, at]
        dy_i = dy[0, :, at].astype(F32)
        s_i = sin[i]
        back = tail_e[:, at] * mm(b, g)
        v = dxs[0, :, at] + back
        dact[:, at] = step_e[:, at] * v + skip[:, at] * dy_i
        part = matrix[:, at]
        q1 = q1 + gather_heads(dy_i * grown[:, at] * mm(c, s_i), part)
        q2 = q2 + gather_heads(x * v, part)
        qb = qb + gather_heads(x * back, part)
        flow = d_e[:, at] * jnp.sum(g.astype(F32) * s_i.astype(F32), axis=0, keepdims=True)
        flows = flows + gather_heads(jnp.broadcast_to(flow, (8, LANE)), part)
        skip_i = jnp.sum(dy_i * x, axis=0, keepdims=True)
        skips = skips + gather_heads(jnp.broadcast_to(skip_i, (8, LANE)), part)
        db = db + mm_nt(tail_e[:, at] * step_e[:, at] * x, g)
        dc = dc + mm_nt(dy_i * grown[:, at], s_i)
    dact[:, inner : inner + LANE] = db
    dact[:, inner + LANE : inner + 2 * LANE] = dc
    shifted, _, rate = steps(dt[0].astype(F32), hp)
    later = jnp.dot(tri(rows, True), q1, precision=HI, preferred_element_type=F32)
    strict = 1.0 - tri(rows, True)
    sooner = jnp.dot(strict, step_v * qb, precision=HI, preferred_element_type=F32)
    da = later + sooner + flows[0:1, :]
    ddt = (q2 + rate * da) * sigmoid(shifted)
    ddt_o[0] = ddt.astype(BF16)
    row = lax.broadcasted_iota(jnp.int32, (8, LANE), 0)
    g_bias = jnp.sum(ddt, axis=0, keepdims=True)
    g_rate = jnp.sum(da * step_v, axis=0, keepdims=True) * rate
    head_o[0] = jnp.where(
        row == 0, g_bias, jnp.where(row == 1, g_rate, jnp.where(row == 2, skips, 0.0))
    )
    buf[0:TAIL, :] = halo[0].astype(F32)
    buf[TAIL : TAIL + rows, :] = xbc[0].astype(F32)
    pre = conv_pre(buf, cw, cb, taps, rows)
    sg = sigmoid(pre)
    dpre = dact[...] * (sg * (1.0 + pre * (1.0 - sg)))
    dpre_o[0] = dpre
    conv_o[0] = jnp.zeros(conv_o.shape[1:], F32)
    for k in range(taps):
        start = TAIL - (taps - 1) + k
        conv_o[0, k : k + 1, :] = jnp.sum(
            dpre * buf[start : start + rows, :], axis=0, keepdims=True
        )
    conv_o[0, taps : taps + 1, :] = jnp.sum(dpre, axis=0, keepdims=True)


def conv_back_kernel(taps, dpre, after, gz, ddt, cw, out, buf):
    rows, chan = dpre.shape[1], dpre.shape[2]
    inner = gz.shape[2]
    buf[0:rows, :] = dpre[0]
    buf[rows : rows + 8, :] = after[0]
    total = cw[taps - 1 : taps, :] * buf[0:rows, :]
    for k in range(taps - 1):
        start = taps - 1 - k
        total = total + cw[k : k + 1, :] * buf[start : start + rows, :]
    out[0, :, 0:inner] = gz[0]
    out[0, :, inner : inner + chan] = total.astype(BF16)
    out[0, :, inner + chan : inner + chan + LANE] = ddt[0]


def per_seq(shape):
    block = (shape[0] // 2,) + shape[1:]
    return pl.BlockSpec(block, lambda s: (s,) + (0,) * (len(shape) - 1))


def same(shape):
    return pl.BlockSpec(shape, lambda s: (0,) * len(shape))


def run(kernel, ins, outs, scratch=(), shared=()):
    return pl.pallas_call(
        kernel,
        grid=(2,),
        in_specs=[(same if n in shared else per_seq)(a.shape) for n, a in enumerate(ins)],
        out_specs=[per_seq(o.shape) for o in outs],
        out_shape=list(outs),
        scratch_shapes=list(scratch),
        compiler_params=pltpu.CompilerParams(vmem_limit_bytes=40 * 2**20),
    )(*ins)


def sds(shape, dtype):
    return jax.ShapeDtypeStruct(shape, dtype)


def prefix(r, decay, reverse, states):
    pieces = r.shape[0]
    out = sds((pieces, states, LANE), BF16)
    params = pltpu.CompilerParams(vmem_limit_bytes=40 * 2**20)
    if decay is None:
        return pl.pallas_call(
            functools.partial(prefix_kernel, reverse, True),
            out_shape=[sds((pieces, LANE), F32), out],
            compiler_params=params,
        )(r)
    return decay, pl.pallas_call(
        functools.partial(prefix_kernel, reverse, False), out_shape=out, compiler_params=params
    )(r, decay)


def exchange(x):
    return lax.all_to_all(x, "seq", split_axis=0, concat_axis=0, tiled=True)


def forward(u, w_in, w_out, p):
    gain_in, cw, cb, hp, gain_out = p
    seqs, rows, width = u.shape
    chan = cw.shape[1]
    taps = 4
    inner = gain_out.shape[1]
    states = LANE
    heads = inner // HDIM
    uf = u.astype(F32)
    inv = lax.rsqrt(jnp.mean(uf * uf, axis=-1, keepdims=True) + EPS)
    normed = (uf * inv * gain_in).astype(BF16).reshape(seqs * rows, width)
    proj = jnp.dot(normed, w_in, preferred_element_type=F32).reshape(seqs, rows, -1)
    z = proj[:, :, :inner]
    xbc = proj[:, :, inner : inner + chan].astype(BF16)
    dt = jnp.pad(
        proj[:, :, inner + chan : inner + chan + heads].astype(BF16),
        ((0, 0), (0, 0), (0, LANE - heads)),
    )
    halo = shift(xbc[:, rows - TAIL :], "seq", 1)
    act, cum, step, sloc = run(
        functools.partial(chunk_kernel, taps),
        (xbc, halo, dt, cw, cb, hp),
        (
            sds((seqs, rows, chan), F32),
            sds((seqs, rows, LANE), F32),
            sds((seqs, rows, LANE), F32),
            sds((seqs * inner // LANE, states + TAIL, LANE), BF16),
        ),
        [pltpu.VMEM((TAIL + rows, chan), F32)],
        (3, 4, 5),
    )
    moved = exchange(sloc)
    (yi,) = run(intra_kernel, (act, cum, step), (sds((seqs, rows, inner), F32),))
    decay, states_in = prefix(moved, None, False, states)
    sin = exchange(states_in)
    yy, gg, ss = run(
        finish_kernel,
        (act, cum, yi, sin, z, hp, gain_out),
        (
            sds((seqs, rows, inner), F32),
            sds((seqs, rows, inner), BF16),
            sds((seqs, rows, 1), F32),
        ),
        (),
        (5, 6),
    )
    mine = jnp.dot(gg.reshape(seqs * rows, inner), w_out, preferred_element_type=F32)
    mine = mine.astype(BF16).reshape(seqs, rows, width)
    theirs, ss_theirs = swap(mine), swap(ss)
    branch = mine.astype(F32) + theirs.astype(F32)
    rn = lax.rsqrt((ss + ss_theirs) * (1.0 / (2 * inner)) + EPS)
    result = (uf + rn * branch).astype(BF16)
    kept = (u, inv, normed, z, xbc, halo, dt, act, cum, step, decay, sin, yy, branch, rn)
    return result, kept


def backward(e, kept, w_in, w_out, p):
    gain_in, cw, cb, hp, gain_out = p
    u, inv, normed, z, xbc, halo, dt, act, cum, step, decay, sin, yy, branch, rn = kept
    seqs, rows, width = e.shape
    chan = cw.shape[1]
    taps = 4
    inner = gain_out.shape[1]
    states = LANE
    ef = e.astype(F32)
    e2 = e.reshape(seqs * rows, width)
    nt = (((1,), (1,)), ((), ()))
    tn = (((0,), (0,)), ((), ()))
    gr = lax.dot_general(e2, w_out, nt, preferred_element_type=F32).reshape(seqs, rows, inner)
    rs = jnp.sum(ef * branch, axis=-1, keepdims=True)
    dy, gz, dsl, dgain, gated = run(
        gate_back_kernel,
        (gr, z, yy, act, cum, rn, rs, hp, gain_out),
        (
            sds((seqs, rows, inner), BF16),
            sds((seqs, rows, inner), BF16),
            sds((seqs * inner // LANE, states, LANE), BF16),
            sds((seqs, 8, inner), F32),
            sds((seqs, rows, inner), BF16),
        ),
        (),
        (7, 8),
    )
    moved = exchange(dsl)
    dxs, dbc, dci = run(
        intra_back_kernel,
        (act, cum, step, dy),
        (
            sds((seqs, rows, inner), F32),
            sds((seqs, rows, 2 * LANE), F32),
            sds((seqs, rows, LANE), F32),
        ),
    )
    _, grads_in = prefix(moved, decay, True, states)
    grad = exchange(grads_in)
    dpre, ddt, conv_g, head_g = run(
        functools.partial(mix_back_kernel, taps),
        (xbc, halo, dt, cw, cb, hp, act, cum, step, dy, dxs, dbc, dci, grad, sin),
        (
            sds((seqs, rows, chan), F32),
            sds((seqs, rows, LANE), BF16),
            sds((seqs, 8, chan), F32),
            sds((seqs, 8, LANE), F32),
        ),
        [pltpu.VMEM((TAIL + rows, chan), F32), pltpu.VMEM((rows, chan), F32)],
        (3, 4, 5),
    )
    after = shift(dpre[:, :8], "seq", -1)
    (gp,) = run(
        functools.partial(conv_back_kernel, taps),
        (dpre, after, gz, ddt, cw),
        (sds((seqs, rows, inner + chan + LANE), BF16),),
        [pltpu.VMEM((rows + 8, chan), F32)],
        (4,),
    )
    gp = gp.reshape(seqs * rows, -1)[:, : w_in.shape[1]]
    mine = lax.dot_general(gp, w_in, nt, preferred_element_type=F32)
    mine = mine.astype(BF16).reshape(seqs, rows, width)
    theirs = swap(mine)
    gn = mine.astype(F32) + theirs.astype(F32)
    uf = u.astype(F32)
    unit = uf * inv
    g_gain_in = jnp.sum(gn * unit, axis=(0, 1))
    scaled = gn * gain_in
    dot = jnp.mean(scaled * unit, axis=-1, keepdims=True)
    grad_u = ef + inv * (scaled - unit * dot)
    g_in = lax.dot_general(normed, gp, tn, preferred_element_type=F32)
    g_out = lax.dot_general(
        gated.reshape(seqs * rows, inner), e2, tn, preferred_element_type=F32
    )
    products = jnp.concatenate([g_in, g_out], axis=1).astype(BF16)
    heads = inner // HDIM
    conv_sum, head_sum = conv_g.sum(0), head_g.sum(0)
    smalls = (
        g_gain_in,
        conv_sum[: taps + 1, :inner],
        conv_sum[: taps + 1, inner:],
        head_sum[:3, :heads],
        dgain.sum(0)[0],
    )
    return grad_u, products, smalls


def body(
    hidden, out_grad, norm_gain, in_weight, conv_weight, conv_bias, dt_bias, a_log, d_skip,
    out_gain, out_weight,
):
    core = lax.axis_index("section")
    width = hidden.shape[2]
    full = out_gain.shape[1]
    taps = conv_weight.shape[1]
    head_count = dt_bias.shape[1]
    proj = in_weight.shape[2]
    bc_at, dt_at = 2 * full, proj - head_count

    wi, wo = in_weight[0], out_weight[0]

    def pack(which):
        out_rows = wo.reshape(2, wo.shape[0] // 2, wo.shape[1])
        return jnp.concatenate(
            [
                half(wi[:, :full], which),
                half(wi[:, full:bc_at], which),
                wi[:, bc_at:dt_at],
                half(wi[:, dt_at:], which),
            ],
            axis=1,
        ), lax.dynamic_index_in_dim(out_rows, which, 0, keepdims=False)

    own, sent = pack(core), pack(1 - core)
    came = jax.tree.map(swap, sent)
    sizes = (norm_gain, conv_weight, conv_bias, dt_bias, a_log, d_skip, out_gain)
    flat = jnp.concatenate([a[0].reshape(-1) for a in sizes])
    flat_other = swap(flat)

    def params(layer):
        mine = core == layer
        w_in = jnp.where(mine, own[0], came[0])
        w_out = jnp.where(mine, own[1], came[1])
        w_in = lax.all_gather(w_in, "wshard", axis=0, tiled=True)
        w_out = lax.all_gather(w_out, "wshard", axis=0, tiled=True)
        v = jnp.where(mine, flat, flat_other)
        parts, at = [], 0
        for a in sizes:
            count = a[0].size
            parts.append(v[at : at + count].reshape(a[0].shape))
            at += count
        gain_in, cw, cb, dtb, al, ds, gain_out = parts

        def channels(a):
            return jnp.concatenate([half(a[..., :full], core), a[..., full:]], axis=-1)

        hp = jnp.stack([half(a, core) for a in (dtb, al, ds)])
        hp = jnp.pad(hp, ((0, 5), (0, LANE - hp.shape[1])))
        cw = jnp.pad(channels(cw), ((0, 8 - taps), (0, 0)))
        return w_in, w_out, (
            gain_in[None],
            cw,
            channels(cb)[None],
            hp,
            half(gain_out, core)[None],
        )

    w_in0, w_out0, p0 = params(0)
    w_in1, w_out1, p1 = params(1)
    first, kept0 = forward(hidden, w_in0, w_out0, p0)
    second, kept1 = forward(first, w_in1, w_out1, p1)
    layer_out = jnp.where(core == 0, first, second)[None]
    grad1, products1, smalls1 = backward(out_grad, kept1, w_in1, w_out1, p1)
    passed = grad1.astype(BF16)
    grad0, products0, smalls0 = backward(passed, kept0, w_in0, w_out0, p0)
    section_grad = jnp.where(core == 0, grad0, passed.astype(F32))[None]

    columns = products0.shape[1]

    def owned(products):
        part = lax.psum_scatter(products, "wshard", scatter_dimension=0, tiled=True)
        part = part.astype(BF16)
        return part

    seq_count = lax.axis_size("seq")
    rows = width // lax.axis_size("wshard") // seq_count
    both = jnp.concatenate(
        [owned(p).reshape(seq_count, rows, columns) for p in (products0, products1)], axis=1
    )
    moved = exchange(both)
    piece = moved.astype(F32).sum(0).astype(BF16).reshape(2, rows, columns)
    mine = lax.dynamic_index_in_dim(piece, core, 0, keepdims=False)
    other = swap(lax.dynamic_index_in_dim(piece, 1 - core, 0, keepdims=False))
    inner = full // 2
    at = (0, inner, 2 * inner, 2 * inner + (dt_at - bc_at), columns - width, columns)
    cut_mine = [mine[:, a:b] for a, b in zip(at, at[1:])]
    cut_other = [other[:, a:b] for a, b in zip(at, at[1:])]
    zg, xg, dg = (whole(cut_mine[n], cut_other[n], core) for n in (0, 1, 3))
    bcg = (cut_mine[2].astype(F32) + cut_other[2].astype(F32)).astype(BF16)
    low_half = jnp.where(core == 0, cut_mine[4], cut_other[4])
    high_half = jnp.where(core == 0, cut_other[4], cut_mine[4])
    ready = jnp.concatenate([zg, xg, bcg, dg, low_half, high_half], axis=1)
    everyone = lax.all_gather(ready, "seq", axis=0, tiled=True)
    grad_w_in = everyone[:, :proj].astype(F32)
    grad_w_out = jnp.concatenate(
        [everyone[:, proj : proj + width], everyone[:, proj + width :]], axis=0
    ).astype(F32)

    small_mine = jax.tree.map(lambda a, b: jnp.where(core == 0, a, b), smalls0, smalls1)
    small_send = jax.tree.map(lambda a, b: jnp.where(core == 0, b, a), smalls0, smalls1)
    shapes = [a.shape for a in small_send]
    flat_send = swap(jnp.concatenate([a.reshape(-1) for a in small_send]))
    small_other, pos = [], 0
    for shape in shapes:
        count = 1
        for n in shape:
            count *= n
        small_other.append(flat_send[pos : pos + count].reshape(shape))
        pos += count
    vector = jnp.concatenate(
        [
            small_mine[0],
            jnp.concatenate(
                [
                    whole(small_mine[1], small_other[1], core),
                    small_mine[2] + small_other[2],
                ],
                axis=1,
            ).reshape(-1),
            whole(small_mine[3], small_other[3], core).reshape(-1),
            whole(small_mine[4], small_other[4], core),
        ]
    )
    share = -(-vector.size // (seq_count * 1024)) * 1024
    vector = jnp.pad(vector, (0, seq_count * share - vector.size)).reshape(seq_count, share)
    part = exchange(vector).sum(0)
    parts = lax.all_gather(part, ("seq", "wshard"), axis=0)
    vector = parts.reshape(seq_count, -1, share).sum(1).reshape(-1)
    chan = full + dt_at - bc_at
    cuts = (width, taps * chan, chan, head_count, head_count, head_count, full)
    small, pos = [], 0
    for count in cuts:
        small.append(vector[pos : pos + count])
        pos += count
    return (
        layer_out,
        section_grad,
        small[0][None],
        grad_w_in[None],
        small[1].reshape(1, taps, chan),
        small[2][None],
        small[3][None],
        small[4][None],
        small[5][None],
        small[6][None],
        grad_w_out[None],
    )


def solution(mesh):
    by_layer = P("section", None)
    weights = P("section", "wshard", None)
    tokens = P("wshard", "seq", None)
    stacked = P("section", "wshard", "seq", None)
    conv = P("section", None, None)
    in_specs = (
        tokens, tokens, by_layer, weights, conv, by_layer, by_layer, by_layer, by_layer, by_layer,
        weights,
    )
    out_specs = (
        stacked, stacked, by_layer, weights, conv, by_layer, by_layer, by_layer, by_layer,
        by_layer, weights,
    )
    return jax.shard_map(body, mesh=mesh, in_specs=in_specs, out_specs=out_specs, check_vma=False)
```

time: 2180 us -> 752 us (0.34)
  local copies, waits for them, and re-layouts: 474 us -> 76.6 us
  waiting for transfers between devices: 520 us -> 192 us
  other arithmetic: 343 us -> 38.8 us
  matrix products: 341 us -> 37.5 us
  blocking collectives: 378 us -> 294 us
  Pallas kernels: 0 us -> 54.4 us
  starting transfers between devices: 81.8 us -> 32.9 us
    psum x1 -> x0, blocking collectives: 348 us -> none  [body(): lax.psum((grad_gain_in, conv_grad_full, bias_grad_full, shift_full, rate_...]
    dot_general x374 -> x12, matrix products: 341 us -> 37.5 us  [the longest x2 10.7 us: forward(): jnp.dot(normed, w_in, preferred_element_type=F32).reshape(seqs, rows, -1)]
    dynamic_update_slice x100 -> x0, local copies, waits for them, and re-layouts: 202 us -> none  [the longest x96 202 us: scan_blocks(): lax.scan(jax.checkpoint(advance), zero_state, (x_blocks, step_blocks, b_b...]
    all_gather x0 -> x1, blocking collectives: none -> 173 us  [body(): parts = lax.all_gather(part, ('seq', 'wshard'), axis=0)]
    another operation x293 -> x2, other arithmetic: 166 us -> 0.02 us  [params(): hp = jnp.stack([half(a, core) for a in (dtb, al, ds)])]
    unnamed x14 -> x7, waiting for transfers between devices: 164 us -> 1.17 us
    all_to_all x2 -> x5, blocking collectives: 29.8 us -> 121 us  [exchange(): return lax.all_to_all(x, 'seq', split_axis=0, concat_axis=0, tiled=True)]
    all_to_all x16 -> x5, waiting for transfers between devices: 96.8 us -> 22.1 us  [exchange(): return lax.all_to_all(x, 'seq', split_axis=0, concat_axis=0, tiled=True)]
  transfers between devices with their start and end apart: 31 -> 27, of which waited for: 25 -> 19; matrix products, arithmetic and copies ran while one was open for 9% -> 9% of each run, Pallas kernels for 0% -> 5%
where the time goes in v1:
time: 752 us; the launch traced here: 743 us
  blocking collectives  294 us (39%)
  waiting for transfers between devices  192 us (26%)
  local copies, waits for them, and re-layouts  76.6 us (10%)
  Pallas kernels  54.4 us (7%)
  other arithmetic  38.8 us (5%)
  matrix products  37.5 us (5%)
  starting transfers between devices  32.9 us (4%)
  between operations  16.6 us (2%)
    all_gather x1, blocking collectives, body(): parts = lax.all_gather(part, ('seq', 'wshard'), axis=0)  173 us
    all_to_all x5, blocking collectives, exchange(): return lax.all_to_all(x, 'seq', split_axis=0, concat_axis=0, tiled=True)  121 us
    all_gather x2, waiting for transfers between devices, params(): w_in = lax.all_gather(w_in, 'wshard', axis=0, tiled=True)  81.7 us
    reduce_scatter x2, waiting for transfers between devices, owned(): part = lax.psum_scatter(products, 'wshard', scatter_dimension=0, tiled=True)  63.2 us
    pallas_call x14, Pallas kernels, run(): pl.pallas_call(kernel, grid=(2,), in_specs=[(same if n in shared else per...  53.1 us
    unnamed x266, local copies, waits for them, and re-layouts  46.3 us
    all_to_all x5, waiting for transfers between devices, exchange(): return lax.all_to_all(x, 'seq', split_axis=0, concat_axis=0, tiled=True)  22.1 us
    all_to_all x5, starting transfers between devices, exchange(): return lax.all_to_all(x, 'seq', split_axis=0, concat_axis=0, tiled=True)  19.8 us
  transfers between devices with their start and end apart: 27, of which 19 were waited for; matrix products, arithmetic and copies ran while one was open for 9% of the time, Pallas kernels for 5%

profile of v1, /device:TPU:0, one launch (start us, length us, event | category | flops | bytes accessed | tf_op | source)
XLA Modules:
  0.0 742.5 jit_solution(12688702935377583947)
XLA Ops:
  24.8 51.7 %all-gather.7.cloned.1.call-done = bf16[1024,2320]{0,1:T(8,128)(2,1)} async-done(((bf16[256,2320]{0,1:T(8,128)(2,1)}), bf16[1024,2320]{0,1:T(8,128)(2,1)}) %all-gather.7.cloned.1.call-update) | async-done | bytes 4751376 | tf_op jit(solution)/shard_map/all_gather | solution.py:561
  76.5 5.4 fusion.55
  90.3 18.2 %all_to_all.54.r = bf16[16,144,128]{2,1,0:T(8,128)(2,1)S(1)} all-to-all(bf16[16,144,128]{2,1,0:T(8,128)(2,1)S(1)} %get-tuple-element.56), channel_id=1, replica_groups=mesh['section'=2,'seq'=16,'wshard'=4] {'seq'}, dimensions={0} | all-to-all | bytes 1179648 | tf_op jit(solution)/shard_map/all_to_all | solution.py:379
  110.0 4.2 all-to-all-start.1
  118.8 5.6 all-to-all-done.1.sin
  138.8 30.0 %all-gather.11.cloned.1.call-done = bf16[1024,2320]{0,1:T(8,128)(2,1)} async-done(((bf16[256,2320]{0,1:T(8,128)(2,1)}), bf16[1024,2320]{0,1:T(8,128)(2,1)}) %all-gather.11.cloned.1.call-update) | async-done | bytes 4751376 | tf_op jit(solution)/shard_map/all_gather | solution.py:561
  168.8 5.4 fusion.56
  183.5 18.2 %all_to_all.55.r = bf16[16,144,128]{2,1,0:T(8,128)(2,1)S(1)} all-to-all(bf16[16,144,128]{2,1,0:T(8,128)(2,1)S(1)} %get-tuple-element.63), channel_id=1, replica_groups=mesh['section'=2,'seq'=16,'wshard'=4] {'seq'}, dimensions={0} | all-to-all | bytes 1179648 | tf_op jit(solution)/shard_map/all_to_all | solution.py:379
  203.2 4.2 all-to-all-start.3
  245.0 16.0 %all_to_all.56.r = bf16[16,128,128]{2,1,0:T(8,128)(2,1)S(1)} all-to-all(bf16[16,128,128]{2,1,0:T(8,128)(2,1)S(1)} %get-tuple-element.72), channel_id=1, replica_groups=mesh['section'=2,'seq'=16,'wshard'=4] {'seq'}, dimensions={0} | all-to-all | bytes 1048576 | tf_op jit(solution)/shard_map/all_to_all | solution.py:379
  261.9 4.2 all-to-all-start.5
  286.2 11.7 %shard_map.205 = (f32[2,128,1280]{2,1,0:T(8,128)S(1)}, bf16[2,128,128]{2,1,0:T(8,128)(2,1)S(1)}, f32[2,8,1280]{2,1,0:T(8,128)S(1)}, f32[2,8,128]{2,1,0:T(8,128)S(1)}) custom-call(bf16[2,128,1280]{2,1,0:T(8,128)(2,1)S(1)} %copy-done.6, bf16[2,16,1280]{2,1,0:T(8,128)(2,1)S(1)} %copy-done.55, bf16[2,128,128]{2,1,0:T(8,128)(2,1)S(1)} %copy-done.39, ...), custom_call_target="tpu_custom_call" | custom-call | tf_op jit(solution)/shard_map/pallas_call | solution.py:348
  300.2 4.2 collective-permute-done.9.after
  305.6 3.6 convolution_convert_fusion
  309.2 6.0 pad_maximum_fusion.1
  315.2 4.0 convolution_convert_fusion.3
  331.6 18.2 %all_to_all.57.r = bf16[16,128,128]{2,1,0:T(8,128)(2,1)S(1)} all-to-all(bf16[16,128,128]{2,1,0:T(8,128)(2,1)S(1)} %get-tuple-element.82), channel_id=1, replica_groups=mesh['section'=2,'seq'=16,'wshard'=4] {'seq'}, dimensions={0} | all-to-all | bytes 1048576 | tf_op jit(solution)/shard_map/all_to_all | solution.py:379
  350.8 3.6 all-to-all-start.7
  360.3 4.8 all-to-all-done.7.grad
  368.3 11.7 %shard_map.210 = (f32[2,128,1280]{2,1,0:T(8,128)S(1)}, bf16[2,128,128]{2,1,0:T(8,128)(2,1)S(1)}, f32[2,8,1280]{2,1,0:T(8,128)S(1)}, f32[2,8,128]{2,1,0:T(8,128)S(1)}) custom-call(bf16[2,128,1280]{2,1,0:T(8,128)(2,1)S(1)} %slice.377.xbc, bf16[2,16,1280]{2,1,0:T(8,128)(2,1)S(1)} %copy-done.53, bf16[2,128,128]{2,1,0:T(8,128)(2,1)S(1)} %copy-done.37, ...), custom_call_target="tpu_custom_call" | custom-call | tf_op jit(solution)/shard_map/pallas_call | solution.py:348
  382.4 4.0 collective-permute-done.11.after
  387.6 3.6 convolution_convert_fusion.1
  391.2 6.0 pad_maximum_fusion
  397.2 3.8 copy.157
  401.0 63.2 %reduce-scatter.3.cloned.1.call-done = bf16[256,3344]{0,1:T(8,128)(2,1)} async-done(((bf16[1024,3344]{0,1:T(8,128)(2,1)}), bf16[256,3344]{0,1:T(8,128)(2,1)}) %reduce-scatter.3.cloned.1.call-update) | async-done | bytes 1712144 | tf_op jit(solution)/shard_map/reduce_scatter | solution.py:598
  464.2 3.8 copy.155
  470.3 50.8 %all_to_all.58 = bf16[16,32,3344]{2,1,0:T(8,128)(2,1)} all-to-all(bf16[16,32,3344]{2,1,0:T(8,128)(2,1)S(1)} %pad_maximum_fusion.2), channel_id=1, replica_groups=mesh['section'=2,'seq'=16,'wshard'=4] {'seq'}, dimensions={0} | all-to-all | bytes 6848512 | tf_op jit(solution)/shard_map/all_to_all | solution.py:379
  528.1 3.9 convolution_convert_fusion.2
  537.2 3.5 all-to-all-start.8
  542.2 6.2 all-to-all-done.8
  548.4 172.9 %all-gather = f32[65536]{0:T(1024)S(1)} all-gather(f32[1024]{0:T(1024)S(1)} %reduce_sum.170), channel_id=2, replica_groups=mesh['section'=2,'seq'=16,'wshard'=4] {'seq','wshard'}, dimensions={0}, use_global_device_ids=true | all-gather | bytes 266240 | tf_op jit(solution)/shard_map/all_gather | solution.py:654
  728.8 4.2 bitcast_convert_fusion.2
  (506 shorter events, 169.3 us)
Async XLA Ops:
  7.2 69.3 %all-gather.7.cloned.1.call-start = ((), (), s32[]{:S(2)}) async-start(), calls=%async_computation.12 | async-start | bytes 5939200 | tf_op jit(solution)/shard_map/all_gather | solution.py:561
  10.8 3.1 collective-permute-start.1
  17.2 113.3 %all-gather.9.cloned.1.call-start = ((), (), s32[]{:S(2)}) async-start(), calls=%async_computation.13 | async-start | bytes 2621440 | tf_op jit(solution)/shard_map/all_gather | solution.py:562
  17.4 2.0 collective-permute-start.4
  20.4 148.3 %all-gather.11.cloned.1.call-start = ((), (), s32[]{:S(2)}) async-start(), calls=%async_computation.14 | async-start | bytes 5939200 | tf_op jit(solution)/shard_map/all_gather | solution.py:561
  21.4 1.3 collective-permute-start
  21.7 60.1 %copy-start.119 = (f32[2,128]{1,0:T(2,128)}, f32[2,128]{1,0:T(2,128)S(1)}, u32[]{:S(2)}) copy-start(f32[2,128]{1,0:T(2,128)S(1)} %add_rsqrt_fusion.3) | copy-start | bytes 3076
  22.7 59.1 %copy-start.114 = (f32[1024]{0:T(1024)}, f32[1024]{0:T(1024)S(1)}, u32[]{:S(2)}) copy-start(f32[1024]{0:T(1024)S(1)} %slice.372) | copy-start | bytes 12292
  23.7 90.7 %copy-start.113 = (f32[4,2304]{1,0:T(4,128)}, f32[4,2304]{1,0:T(4,128)S(1)}, u32[]{:S(2)}) copy-start(f32[4,2304]{1,0:T(4,128)S(1)} %reshape.639) | copy-start | bytes 110596
  24.6 62.7 %copy-start.32 = (f32[8,1280]{1,0:T(8,128)}, f32[8,1280]{1,0:T(8,128)S(1)}, u32[]{:S(2)}) copy-start(f32[8,1280]{1,0:T(8,128)S(1)} %select_maximum_fusion.1.cw) | copy-start | bytes 122884
  24.8 57.0 %copy-start.101 = (bf16[2,128,1024]{2,1,0:T(8,128)(2,1)}, bf16[2,128,1024]{2,1,0:T(8,128)(2,1)S(1)}, u32[]{:S(2)}) copy-start(bf16[2,128,1024]{2,1,0:T(8,128)(2,1)S(1)} %fusion.23) | copy-start | bytes 1572868
  81.8 5.4 collective-permute-start.2
  110.0 14.4 %all-to-all-start.1 = ((bf16[16,128,128]{2,1,0:T(8,128)(2,1)}), bf16[16,128,128]{2,1,0:T(8,128)(2,1)}, u32[]{:S(2)}, u32[]{:S(2)}) async-start(bf16[16,128,128]{2,1,0:T(8,128)(2,1)} %get-tuple-element.57), calls=%async_computation.1 | async-start | bytes 1048576 | tf_op jit(solution)/shard_map/all_to_all | solution.py:379
  114.3 111.9 %all-gather.13.cloned.1.call-start = ((), (), s32[]{:S(2)}) async-start(), calls=%async_computation.15 | async-start | bytes 2621440 | tf_op jit(solution)/shard_map/all_gather | solution.py:562
  133.0 3.4 collective-permute-start.5
  133.8 1.9 collective-permute-start.3
  174.2 5.4 collective-permute-start.6
  203.2 14.4 %all-to-all-start.3 = ((bf16[16,128,128]{2,1,0:T(8,128)(2,1)}), bf16[16,128,128]{2,1,0:T(8,128)(2,1)}, u32[]{:S(2)}, u32[]{:S(2)}) async-start(bf16[16,128,128]{2,1,0:T(8,128)(2,1)} %copy-done.47), calls=%async_computation.3 | async-start | bytes 1048576 | tf_op jit(solution)/shard_map/all_to_all | solution.py:379
  228.8 3.6 collective-permute-start.8
  228.9 2.2 collective-permute-start.7
  261.9 15.0 %all-to-all-start.5 = ((bf16[16,128,128]{2,1,0:T(8,128)(2,1)}), bf16[16,128,128]{2,1,0:T(8,128)(2,1)}, u32[]{:S(2)}, u32[]{:S(2)}) async-start(bf16[16,128,128]{2,1,0:T(8,128)(2,1)} %copy-done.16), calls=%async_computation.5 | async-start | bytes 1048576 | tf_op jit(solution)/shard_map/all_to_all | solution.py:379
  266.1 131.1 %reduce-scatter.5.cloned.1.call-start = ((), (), s32[]{:S(2)}) async-start(), calls=%async_computation.17 | async-start | bytes 8560640 | tf_op jit(solution)/shard_map/reduce_scatter | solution.py:598
  297.9 6.5 collective-permute-start.9
  319.2 2.2 collective-permute-start.10
  350.8 14.3 %all-to-all-start.7 = ((bf16[16,128,128]{2,1,0:T(8,128)(2,1)}), bf16[16,128,128]{2,1,0:T(8,128)(2,1)S(1)}, u32[]{:S(2)}, u32[]{:S(2)}) async-start(bf16[16,128,128]{2,1,0:T(8,128)(2,1)} %copy-done.17), calls=%async_computation.7 | async-start | bytes 1048576 | tf_op jit(solution)/shard_map/all_to_all | solution.py:379
  354.4 109.8 %reduce-scatter.3.cloned.1.call-start = ((), (), s32[]{:S(2)}) async-start(), calls=%async_computation.16 | async-start | bytes 8560640 | tf_op jit(solution)/shard_map/reduce_scatter | solution.py:598
  380.0 6.5 collective-permute-start.11
  397.2 327.5 %all-gather.15.cloned.1.call-start = ((), (), s32[]{:S(2)}) async-start(), calls=%async_computation.18 | async-start | bytes 3551232 | tf_op jit(solution)/shard_map/all_gather | solution.py:620
  523.7 1.4 collective-permute-start.14
  532.1 2.0 collective-permute-start.12
  534.7 1.2 collective-permute-start.13
  537.2 11.1 %all-to-all-start.8 = ((f32[16,1,1024]{2,1,0:T(1,128)}), f32[16,1,1024]{2,1,0:T(1,128)S(1)}, u32[]{:S(2)}, u32[]{:S(2)}) async-start(f32[16,1,1024]{2,1,0:T(1,128)} %bitcast.41), calls=%async_computation.8 | async-start | bytes 131072 | tf_op jit(solution)/shard_map/all_to_all | solution.py:379
  (127 other events, 766.4 us)
Sparse Core Ops, SparseCore 0:
  17.3 59.1 all-gather.6
  78.1 31.6 all-gather.8
  112.0 56.6 all-gather.10
  170.3 31.6 all-gather.12
  315.3 68.4 reduce-scatter.4
  397.3 66.8 reduce-scatter.2
  526.9 44.7 all-gather.14

commit v2 on v1

--- a/solution.py
+++ b/solution.py
@@ -98,14 +98,43 @@
     return pre
 
 
-def chunk_kernel(taps, xbc, halo, dt, cw, cb, hp, act_o, cum_o, step_o, sloc_o, buf):
-    rows, inner = xbc.shape[1], sloc_o.shape[0] * LANE
+MESH = pl.DeviceIdType.MESH
+
+
+class Sender:
+    def __init__(self, send, recv):
+        self.send, self.recv, self.used = send, recv, 0
+
+    def start(self, src, dst, device):
+        n = self.used
+        self.used += 1
+        copy = pltpu.make_async_remote_copy(
+            src_ref=src,
+            dst_ref=dst,
+            send_sem=self.send.at[n],
+            recv_sem=self.recv.at[n],
+            device_id=device,
+            device_id_type=MESH,
+        )
+        copy.start()
+        return copy
+
+
+def greet(devices):
+    barrier = pltpu.get_barrier_semaphore()
+    for device in devices:
+        pl.semaphore_signal(barrier, inc=1, device_id=device, device_id_type=MESH)
+    pl.semaphore_wait(barrier, len(devices))
+
+
+def chunk_kernel(taps, xd, halo, cw, cb, hp, act_o, cum_o, step_o, sloc_o, buf):
+    rows, inner, chan = xd.shape[1], sloc_o.shape[0] * LANE, cw.shape[1]
     buf[0:TAIL, :] = halo[0].astype(F32)
-    buf[TAIL : TAIL + rows, :] = xbc[0].astype(F32)
+    buf[TAIL : TAIL + rows, :] = xd[0, :, 0:chan].astype(F32)
     pre = conv_pre(buf, cw, cb, taps, rows)
     act = pre * sigmoid(pre)
     act_o[0] = act
-    _, step, rate = steps(dt[0].astype(F32), hp)
+    _, step, rate = steps(xd[0, :, chan : chan + LANE].astype(F32), hp)
     cum = jnp.dot(tri(rows, False), step * rate, precision=HI, preferred_element_type=F32)
     cum_o[0] = cum
     step_o[0] = step
@@ -128,21 +157,48 @@
         sloc_o[i, states : states + TAIL, :] = extra[:, i * LANE : (i + 1) * LANE]
 
 
-def prefix_kernel(reverse, with_decay, r, *refs):
-    pieces, states = r.shape[0], refs[-1].shape[1]
+def scan_kernel(reverse, with_decay, pieces_ref, *refs):
     if with_decay:
-        decay_o, out = refs
-        for j in range(pieces):
-            tail = r[j, states : states + TAIL, :].astype(F32)
-            decay_o[j : j + 1, :] = tail[0:1, :] + tail[1:2, :] + tail[2:3, :]
-        decay = decay_o
+        decay, out, got, done, send_a, recv_a, send_b, recv_b = refs
     else:
-        decay, out = refs
+        decay, out, got, done, send_a, recv_a, send_b, recv_b = refs
+    count, states = out.shape[0], out.shape[1]
+    q = lax.axis_index("seq")
+    peers = [lax.rem(q + d, count) for d in range(1, count)]
+    greet([{"seq": p} for p in peers])
+
+    def copy(src, dst, send, recv, n, peer, slot):
+        return pltpu.make_async_remote_copy(
+            src_ref=src.at[peer],
+            dst_ref=dst.at[slot],
+            send_sem=send.at[n],
+            recv_sem=recv.at[slot],
+            device_id={"seq": peer},
+            device_id_type=MESH,
+        )
+
+    sent = [copy(pieces_ref, got, send_a, recv_a, n, p, q) for n, p in enumerate(peers)]
+    for c in sent:
+        c.start()
+    got[q] = pieces_ref[q]
+    for n, p in enumerate(peers):
+        copy(pieces_ref, got, send_a, recv_a, n, p, p).wait_recv()
     carry = jnp.zeros((states, LANE), F32)
-    order = range(pieces - 1, -1, -1) if reverse else range(pieces)
+    order = range(count - 1, -1, -1) if reverse else range(count)
     for j in order:
-        out[j] = carry.astype(BF16)
-        carry = carry * decay[j : j + 1, :] + r[j, 0:states, :].astype(F32)
+        if with_decay:
+            tail = got[j, states : states + TAIL, :].astype(F32)
+            decay[j : j + 1, :] = tail[0:1, :] + tail[1:2, :] + tail[2:3, :]
+        done[j] = carry.astype(BF16)
+        carry = carry * decay[j : j + 1, :] + got[j, 0:states, :].astype(F32)
+    back = [copy(done, out, send_b, recv_b, n, p, q) for n, p in enumerate(peers)]
+    for c in back:
+        c.start()
+    out[q] = done[q]
+    for n, p in enumerate(peers):
+        copy(done, out, send_b, recv_b, n, p, p).wait_recv()
+    for c in sent + back:
+        c.wait_send()
 
 
 def intra_kernel(act, cum, step, yi_o):
@@ -252,10 +308,10 @@
 
 
 def mix_back_kernel(
-    taps, xbc, halo, dt, cw, cb, hp, act, cum, step, dy, dxs, dbc, dci, grad, sin,
+    taps, xd, halo, cw, cb, hp, act, cum, step, dy, dxs, dbc, dci, grad, sin,
     dpre_o, ddt_o, conv_o, head_o, buf, dact,
 ):
-    rows, inner = dy.shape[1], dy.shape[2]
+    rows, inner, chan = dy.shape[1], dy.shape[2], cw.shape[1]
     matrix = spread_matrix(inner)
     cum_v, step_v = cum[0], step[0]
     last = cum_v[rows - 1 : rows, :]
@@ -293,7 +349,7 @@
         dc = dc + mm_nt(dy_i * grown[:, at], s_i)
     dact[:, inner : inner + LANE] = db
     dact[:, inner + LANE : inner + 2 * LANE] = dc
-    shifted, _, rate = steps(dt[0].astype(F32), hp)
+    shifted, _, rate = steps(xd[0, :, chan : chan + LANE].astype(F32), hp)
     later = jnp.dot(tri(rows, True), q1, precision=HI, preferred_element_type=F32)
     strict = 1.0 - tri(rows, True)
     sooner = jnp.dot(strict, step_v * qb, precision=HI, preferred_element_type=F32)
@@ -307,7 +363,7 @@
         row == 0, g_bias, jnp.where(row == 1, g_rate, jnp.where(row == 2, skips, 0.0))
     )
     buf[0:TAIL, :] = halo[0].astype(F32)
-    buf[TAIL : TAIL + rows, :] = xbc[0].astype(F32)
+    buf[TAIL : TAIL + rows, :] = xd[0, :, 0:chan].astype(F32)
     pre = conv_pre(buf, cw, cb, taps, rows)
     sg = sigmoid(pre)
     dpre = dact[...] * (sg * (1.0 + pre * (1.0 - sg)))
@@ -321,18 +377,16 @@
     conv_o[0, taps : taps + 1, :] = jnp.sum(dpre, axis=0, keepdims=True)
 
 
-def conv_back_kernel(taps, dpre, after, gz, ddt, cw, out, buf):
+def conv_back_kernel(taps, dpre, after, ddt, cw, out, buf):
     rows, chan = dpre.shape[1], dpre.shape[2]
-    inner = gz.shape[2]
     buf[0:rows, :] = dpre[0]
     buf[rows : rows + 8, :] = after[0]
     total = cw[taps - 1 : taps, :] * buf[0:rows, :]
     for k in range(taps - 1):
         start = taps - 1 - k
         total = total + cw[k : k + 1, :] * buf[start : start + rows, :]
-    out[0, :, 0:inner] = gz[0]
-    out[0, :, inner : inner + chan] = total.astype(BF16)
-    out[0, :, inner + chan : inner + chan + LANE] = ddt[0]
+    out[0, :, 0:chan] = total.astype(BF16)
+    out[0, :, chan : chan + LANE] = ddt[0]
 
 
 def per_seq(shape):
@@ -360,47 +414,309 @@
     return jax.ShapeDtypeStruct(shape, dtype)
 
 
-def prefix(r, decay, reverse, states):
-    pieces = r.shape[0]
-    out = sds((pieces, states, LANE), BF16)
-    params = pltpu.CompilerParams(vmem_limit_bytes=40 * 2**20)
-    if decay is None:
-        return pl.pallas_call(
-            functools.partial(prefix_kernel, reverse, True),
-            out_shape=[sds((pieces, LANE), F32), out],
-            compiler_params=params,
-        )(r)
-    return decay, pl.pallas_call(
-        functools.partial(prefix_kernel, reverse, False), out_shape=out, compiler_params=params
-    )(r, decay)
-
-
-def exchange(x):
-    return lax.all_to_all(x, "seq", split_axis=0, concat_axis=0, tiled=True)
-
-
-def forward(u, w_in, w_out, p):
+def scan_chunks(pieces, decay, reverse, states):
+    count, height = pieces.shape[0], pieces.shape[1]
+    place = pl.BlockSpec(memory_space=pltpu.VMEM)
+    out = sds((count, states, LANE), BF16)
+    outs = [sds((count, LANE), F32), out] if decay is None else [out]
+    ins = (pieces,) if decay is None else (pieces, decay)
+    sems = [pltpu.SemaphoreType.DMA((count,))] * 4
+    return pl.pallas_call(
+        functools.partial(scan_kernel, reverse, decay is None),
+        out_shape=outs,
+        in_specs=[place] * len(ins),
+        out_specs=[place] * len(outs),
+        scratch_shapes=[
+            pltpu.VMEM((count, height, LANE), BF16),
+            pltpu.VMEM((count, states, LANE), BF16),
+            *sems,
+        ],
+        compiler_params=pltpu.CompilerParams(
+            collective_id=1 + reverse, has_side_effects=True, vmem_limit_bytes=40 * 2**20
+        ),
+    )(*ins)
+
+
+def assemble_kernel(head_count, core, e, l, eo, lo, in_o, out_o):
+    rows, full = e.shape[0], e.shape[1]
+    inner = full // 2
+    wide = 2 * inner // 8
+    bc = l.shape[1] - inner - LANE
+    zero = core[0] == 0
+    for n in range(4):
+        src = slice(n * wide, (n + 1) * wide)
+        for base, a, b in ((0, e, eo), (2 * inner, l, lo)):
+            mine, other = a[:, src].astype(F32), b[:, src].astype(F32)
+            low = base + 2 * n * wide
+            in_o[:, low : low + wide] = jnp.where(zero, mine, other)
+            in_o[:, low + wide : low + 2 * wide] = jnp.where(zero, other, mine)
+    at = slice(inner, inner + bc)
+    in_o[:, 4 * inner : 4 * inner + bc] = l[:, at].astype(F32) + lo[:, at].astype(F32)
+    i = lax.broadcasted_iota(jnp.int32, (LANE, LANE), 0)
+    j = lax.broadcasted_iota(jnp.int32, (LANE, LANE), 1)
+    per = head_count // 8
+    spot = 2 * per * (i // per) + lax.rem(i, per)
+    valid = i < head_count // 2
+    first = jnp.where(valid & (j == spot), 1.0, 0.0)
+    second = jnp.where(valid & (j == spot + per), 1.0, 0.0)
+    at = slice(inner + bc, inner + bc + LANE)
+    heads = mm(l[:, at], jnp.where(zero, first, second)) + mm(
+        lo[:, at], jnp.where(zero, second, first)
+    )
+    in_o[:, 4 * inner + bc : 4 * inner + bc + head_count] = heads[:, 0:head_count]
+    mine, other = e[:, inner:].astype(F32), eo[:, inner:].astype(F32)
+    out_o[0] = jnp.where(zero, mine, other)
+    out_o[1] = jnp.where(zero, other, mine)
+
+
+def assemble(core, early, late, early_o, late_o, proj, head_count):
+    flat = [a.reshape(-1, a.shape[-1]) for a in (early, late, early_o, late_o)]
+    rows, step = flat[0].shape[0], 64
+    inner = flat[0].shape[1] // 2
+    return pl.pallas_call(
+        functools.partial(assemble_kernel, head_count),
+        grid=(rows // step,),
+        in_specs=[pl.BlockSpec(memory_space=pltpu.SMEM)]
+        + [pl.BlockSpec((step, a.shape[1]), lambda r: (r, 0)) for a in flat],
+        out_specs=[
+            pl.BlockSpec((step, proj), lambda r: (r, 0)),
+            pl.BlockSpec((2, step, inner), lambda r: (0, r, 0)),
+        ],
+        out_shape=[sds((rows, proj), F32), sds((2, rows, inner), F32)],
+        compiler_params=pltpu.CompilerParams(vmem_limit_bytes=40 * 2**20),
+    )(core.astype(jnp.int32).reshape(1), *flat)
+
+
+def spread_kernel(x_own, z_own, o_own, x_all, z_all, o_all, send, recv, local):
+    sender = Sender(send, recv)
+    q = lax.axis_index("seq")
+    x = lax.axis_index("wshard")
+    z, y = q // 4, lax.rem(q, 4)
+    shards = [lax.rem(x + d, 4) for d in (1, 2, 3)]
+    z_up, z_down = lax.rem(z + 1, 4), lax.rem(z + 3, 4)
+    y_up, y_down = lax.rem(y + 1, 4), lax.rem(y + 3, 4)
+    to_z_up, to_z_down = {"seq": z_up * 4 + y}, {"seq": z_down * 4 + y}
+    to_y_up, to_y_down = {"seq": z * 4 + y_up}, {"seq": z * 4 + y_down}
+    greet([{"wshard": p} for p in shards] + [to_z_up, to_z_down, to_y_up, to_y_down])
+    pairs = ((x_own, x_all), (z_own, z_all), (o_own, o_all))
+    sent = [
+        sender.start(own.at[z, y], full.at[x, z, y], {"wshard": p})
+        for p in shards
+        for own, full in pairs
+    ]
+    kept = [
+        pltpu.make_async_copy(own, full.at[x], local.at[n]) for n, (own, full) in enumerate(pairs)
+    ]
+    for copy in kept:
+        copy.start()
+    for copy in sent:
+        copy.wait()
+    cut = 384
+    over_y = ((x_all, slice(0, x_all.shape[-1])), (o_all, slice(0, cut)))
+    over_z = ((z_all, slice(0, z_all.shape[-1])), (o_all, slice(cut, o_all.shape[-1])))
+    ups, downs = [], []
+
+    def both_ways(refs, up, down):
+        ups.append([sender.start(r, r, up) for r in refs])
+        downs.append([sender.start(r, r, down) for r in refs])
+
+    for p in shards:
+        both_ways([a.at[p, z, y, :, c] for a, c in over_y], to_y_up, to_y_down)
+        both_ways([a.at[p, z, y, :, c] for a, c in over_z], to_z_up, to_z_down)
+    rest = []
+    for n, p in enumerate(shards):
+        for copy in ups[2 * n] + ups[2 * n + 1] + downs[2 * n] + downs[2 * n + 1]:
+            copy.wait()
+        if n != 1:
+            refs = [a.at[p, z, y_down, :, c] for a, c in over_y[: 2 if n == 0 else 1]]
+            rest += [sender.start(r, r, to_y_up) for r in refs]
+            refs = [a.at[p, z_down, y, :, c] for a, c in over_z[: 2 if n == 0 else 1]]
+            rest += [sender.start(r, r, to_z_up) for r in refs]
+        if n != 0:
+            refs = [a.at[p, z, y_up, :, c] for a, c in over_y[0 if n == 1 else 1 :]]
+            rest += [sender.start(r, r, to_y_down) for r in refs]
+            refs = [a.at[p, z_up, y, :, c] for a, c in over_z[0 if n == 1 else 1 :]]
+            rest += [sender.start(r, r, to_z_down) for r in refs]
+    for copy in rest:
+        copy.wait()
+    ups.clear()
+    downs.clear()
+    for p in shards:
+        both_ways([a.at[p, z, :, :, c] for a, c in over_y], to_z_up, to_z_down)
+        both_ways([a.at[p, :, y, :, c] for a, c in over_z], to_y_up, to_y_down)
+    rest = []
+    low, high = slice(0, 2), slice(2, 4)
+    for n, p in enumerate(shards):
+        for copy in ups[2 * n] + ups[2 * n + 1] + downs[2 * n] + downs[2 * n + 1]:
+            copy.wait()
+        for a, c in over_y:
+            here, there = a.at[p, z_down, low, :, c], a.at[p, z_up, high, :, c]
+            rest += [sender.start(here, here, to_z_up), sender.start(there, there, to_z_down)]
+        for a, c in over_z:
+            here, there = a.at[p, low, y_down, :, c], a.at[p, high, y_up, :, c]
+            rest += [sender.start(here, here, to_y_up), sender.start(there, there, to_y_down)]
+    for copy in rest:
+        copy.wait()
+    for copy in kept:
+        copy.wait()
+
+
+def spread_weights(x_own, z_own, o_own):
+    own = [a.reshape(4, 4, a.shape[0] // 16, a.shape[1]) for a in (x_own, z_own, o_own)]
+    place = pl.BlockSpec(memory_space=pltpu.VMEM)
+    count = 9 + 24 + 12 + 24 + 24
+    full = pl.pallas_call(
+        spread_kernel,
+        out_shape=[sds((4,) + a.shape, BF16) for a in own],
+        in_specs=[place] * 3,
+        out_specs=[place] * 3,
+        scratch_shapes=[
+            pltpu.SemaphoreType.DMA((count,)),
+            pltpu.SemaphoreType.DMA((count,)),
+            pltpu.SemaphoreType.DMA((3,)),
+        ],
+        compiler_params=pltpu.CompilerParams(
+            collective_id=3, has_side_effects=True, vmem_limit_bytes=40 * 2**20
+        ),
+    )(*own)
+    return tuple(a.reshape(-1, a.shape[-1]) for a in full)
+
+
+def reduce_kernel(a0, b0, a1, b1, small, *refs):
+    g_own, g_other = refs[0:3], refs[3:6]
+    xr, xs = refs[6:8]
+    r1, t, r2 = (refs[8:11], refs[11:14]), (refs[14:17], refs[17:20]), (refs[20:23], refs[23:26])
+    f, o = refs[26:29], refs[29:32]
+    sender = Sender(refs[32], refs[33])
+    core = lax.axis_index("section")
+    q = lax.axis_index("seq")
+    x = lax.axis_index("wshard")
+    z, y = q // 4, lax.rem(q, 4)
+
+    def on_x(d):
+        return {"wshard": lax.rem(x + d, 4)}
+
+    def on_y(d):
+        return {"seq": z * 4 + lax.rem(y + d, 4)}
+
+    def on_z(d):
+        return {"seq": lax.rem(z + d, 4) * 4 + y}
+
+    twin = {"section": 1 - core}
+    greet([on(d) for on in (on_x, on_y, on_z) for d in (1, 2, 3)] + [twin])
+
+    def first(layer, arrays, places):
+        copies = []
+        for n, a in zip(places, arrays):
+            for d in (1, 2, 3):
+                if layer == 0:
+                    peer, src = on_y(d), a.at[:, lax.rem(y + d, 4)]
+                else:
+                    peer, src = on_z(d), a.at[lax.rem(z + d, 4)]
+                copies.append(sender.start(src, r1[layer][n].at[d - 1], peer))
+        return copies
+
+    x_copies = [sender.start(small, xr.at[d - 1], on_x(d)) for d in (1, 2, 3)]
+    layers = ((a0, b0, xs.at[0]), (a1, b1, xs.at[1]))
+    copies = [first(layer, layers[layer][0:2], (0, 1)) for layer in (0, 1)]
+    for copy in x_copies:
+        copy.wait()
+    xs[...] = small[...] + xr[0] + xr[1] + xr[2]
+    for layer in (0, 1):
+        copies[layer] += first(layer, layers[layer][2:3], (2,))
+    second = []
+    for layer in (0, 1):
+        for copy in copies[layer]:
+            copy.wait()
+        for n, a in enumerate(layers[layer]):
+            for j in range(4):
+                own = a[j, y] if layer == 0 else a[z, j]
+                total = own.astype(F32)
+                for d in range(3):
+                    total = total + r1[layer][n][d, j].astype(F32)
+                t[layer][n][j] = total.astype(t[layer][n].dtype)
+        for n in range(3):
+            for d in (1, 2, 3):
+                to = lax.rem(z + d, 4) if layer == 0 else lax.rem(y + d, 4)
+                peer = on_z(d) if layer == 0 else on_y(d)
+                second.append(sender.start(t[layer][n].at[to], r2[layer][n].at[d - 1], peer))
+    for copy in second:
+        copy.wait()
+    for layer in (0, 1):
+        for n in range(3):
+            total = t[layer][n][z if layer == 0 else y].astype(F32)
+            for d in range(3):
+                total = total + r2[layer][n][d].astype(F32)
+            f[n][layer] = total.astype(f[n].dtype)
+    twins = [sender.start(f[n].at[1 - core], o[n], twin) for n in range(3)]
+    gather = []
+    for n in range(3):
+        g_own[n][z, y] = f[n][core]
+        for d in (1, 2, 3):
+            gather.append(sender.start(f[n].at[core], g_own[n].at[z, y], on_y(d)))
+    for copy in twins:
+        copy.wait()
+    for n in range(3):
+        g_other[n][z, y] = o[n][...]
+        for d in (1, 2, 3):
+            gather.append(sender.start(o[n], g_other[n].at[z, y], on_z(d)))
+    for copy in gather:
+        copy.wait()
+    gather = []
+    for n in range(3):
+        for d in (1, 2, 3):
+            gather.append(sender.start(g_own[n].at[z], g_own[n].at[z], on_z(d)))
+            gather.append(sender.start(g_other[n].at[:, y], g_other[n].at[:, y], on_y(d)))
+    for copy in gather:
+        copy.wait()
+
+
+def reduce_all(grids, small):
+    kinds = [(a.shape[2:], a.dtype) for a in (grids[0], grids[1], small[0])]
+    full = [sds((4, 4) + shape, dtype) for shape, dtype in kinds]
+
+    def vmem(*lead):
+        return [pltpu.VMEM(lead + shape, dtype) for shape, dtype in kinds]
+
+    scratch = [
+        pltpu.VMEM((3,) + small.shape, F32),
+        pltpu.VMEM(small.shape, F32),
+        *vmem(3, 4), *vmem(3, 4), *vmem(4), *vmem(4), *vmem(3), *vmem(3), *vmem(2), *vmem(),
+        pltpu.SemaphoreType.DMA((3 + 18 + 18 + 3 + 18 + 18,)),
+        pltpu.SemaphoreType.DMA((3 + 18 + 18 + 3 + 18 + 18,)),
+    ]
+    place = pl.BlockSpec(memory_space=pltpu.VMEM)
+    out = pl.pallas_call(
+        reduce_kernel,
+        out_shape=full + full,
+        in_specs=[place] * 5,
+        out_specs=[place] * 6,
+        scratch_shapes=scratch,
+        compiler_params=pltpu.CompilerParams(
+            collective_id=0, has_side_effects=True, vmem_limit_bytes=40 * 2**20
+        ),
+    )(*grids, small)
+    return out[0:3], out[3:6]
+
+
+def forward(u, w, p):
+    w_x, w_z, w_out = w
     gain_in, cw, cb, hp, gain_out = p
     seqs, rows, width = u.shape
     chan = cw.shape[1]
     taps = 4
     inner = gain_out.shape[1]
     states = LANE
-    heads = inner // HDIM
     uf = u.astype(F32)
     inv = lax.rsqrt(jnp.mean(uf * uf, axis=-1, keepdims=True) + EPS)
     normed = (uf * inv * gain_in).astype(BF16).reshape(seqs * rows, width)
-    proj = jnp.dot(normed, w_in, preferred_element_type=F32).reshape(seqs, rows, -1)
-    z = proj[:, :, :inner]
-    xbc = proj[:, :, inner : inner + chan].astype(BF16)
-    dt = jnp.pad(
-        proj[:, :, inner + chan : inner + chan + heads].astype(BF16),
-        ((0, 0), (0, 0), (0, LANE - heads)),
-    )
-    halo = shift(xbc[:, rows - TAIL :], "seq", 1)
+    xd = jnp.dot(normed, w_x, preferred_element_type=F32).astype(BF16)
+    xd = xd.reshape(seqs, rows, chan + LANE)
+    z = jnp.dot(normed, w_z, preferred_element_type=F32).reshape(seqs, rows, inner)
+    halo = shift(xd[:, rows - TAIL :, :chan], "seq", 1)
     act, cum, step, sloc = run(
         functools.partial(chunk_kernel, taps),
-        (xbc, halo, dt, cw, cb, hp),
+        (xd, halo, cw, cb, hp),
         (
             sds((seqs, rows, chan), F32),
             sds((seqs, rows, LANE), F32),
@@ -408,12 +724,10 @@
             sds((seqs * inner // LANE, states + TAIL, LANE), BF16),
         ),
         [pltpu.VMEM((TAIL + rows, chan), F32)],
-        (3, 4, 5),
-    )
-    moved = exchange(sloc)
+        (2, 3, 4),
+    )
     (yi,) = run(intra_kernel, (act, cum, step), (sds((seqs, rows, inner), F32),))
-    decay, states_in = prefix(moved, None, False, states)
-    sin = exchange(states_in)
+    decay, sin = scan_chunks(sloc, None, False, states)
     yy, gg, ss = run(
         finish_kernel,
         (act, cum, yi, sin, z, hp, gain_out),
@@ -431,13 +745,14 @@
     branch = mine.astype(F32) + theirs.astype(F32)
     rn = lax.rsqrt((ss + ss_theirs) * (1.0 / (2 * inner)) + EPS)
     result = (uf + rn * branch).astype(BF16)
-    kept = (u, inv, normed, z, xbc, halo, dt, act, cum, step, decay, sin, yy, branch, rn)
+    kept = (u, inv, normed, z, xd, halo, act, cum, step, decay, sin, yy, branch, rn)
     return result, kept
 
 
-def backward(e, kept, w_in, w_out, p):
+def backward(e, kept, w, p):
+    w_x, w_z, w_out = w
     gain_in, cw, cb, hp, gain_out = p
-    u, inv, normed, z, xbc, halo, dt, act, cum, step, decay, sin, yy, branch, rn = kept
+    u, inv, normed, z, xd, halo, act, cum, step, decay, sin, yy, branch, rn = kept
     seqs, rows, width = e.shape
     chan = cw.shape[1]
     taps = 4
@@ -462,7 +777,18 @@
         (),
         (7, 8),
     )
-    moved = exchange(dsl)
+    gz = gz.reshape(seqs * rows, inner)
+    part_z = lax.dot_general(gz, w_z, nt, preferred_element_type=F32)
+    early = jnp.concatenate(
+        [
+            lax.dot_general(normed, gz, tn, preferred_element_type=F32),
+            lax.dot_general(
+                gated.reshape(seqs * rows, inner), e2, tn, preferred_element_type=F32
+            ),
+        ],
+        axis=1,
+    ).astype(BF16)
+    early = lax.psum_scatter(early, "wshard", scatter_dimension=0, tiled=True)
     dxs, dbc, dci = run(
         intra_back_kernel,
         (act, cum, step, dy),
@@ -472,11 +798,10 @@
             sds((seqs, rows, LANE), F32),
         ),
     )
-    _, grads_in = prefix(moved, decay, True, states)
-    grad = exchange(grads_in)
+    (grad,) = scan_chunks(dsl, decay, True, states)
     dpre, ddt, conv_g, head_g = run(
         functools.partial(mix_back_kernel, taps),
-        (xbc, halo, dt, cw, cb, hp, act, cum, step, dy, dxs, dbc, dci, grad, sin),
+        (xd, halo, cw, cb, hp, act, cum, step, dy, dxs, dbc, dci, grad, sin),
         (
             sds((seqs, rows, chan), F32),
             sds((seqs, rows, LANE), BF16),
@@ -484,18 +809,18 @@
             sds((seqs, 8, LANE), F32),
         ),
         [pltpu.VMEM((TAIL + rows, chan), F32), pltpu.VMEM((rows, chan), F32)],
-        (3, 4, 5),
+        (2, 3, 4),
     )
     after = shift(dpre[:, :8], "seq", -1)
     (gp,) = run(
         functools.partial(conv_back_kernel, taps),
-        (dpre, after, gz, ddt, cw),
-        (sds((seqs, rows, inner + chan + LANE), BF16),),
+        (dpre, after, ddt, cw),
+        (sds((seqs, rows, chan + LANE), BF16),),
         [pltpu.VMEM((rows + 8, chan), F32)],
-        (4,),
-    )
-    gp = gp.reshape(seqs * rows, -1)[:, : w_in.shape[1]]
-    mine = lax.dot_general(gp, w_in, nt, preferred_element_type=F32)
+        (3,),
+    )
+    gp = gp.reshape(seqs * rows, -1)
+    mine = part_z + lax.dot_general(gp, w_x, nt, preferred_element_type=F32)
     mine = mine.astype(BF16).reshape(seqs, rows, width)
     theirs = swap(mine)
     gn = mine.astype(F32) + theirs.astype(F32)
@@ -505,11 +830,8 @@
     scaled = gn * gain_in
     dot = jnp.mean(scaled * unit, axis=-1, keepdims=True)
     grad_u = ef + inv * (scaled - unit * dot)
-    g_in = lax.dot_general(normed, gp, tn, preferred_element_type=F32)
-    g_out = lax.dot_general(
-        gated.reshape(seqs * rows, inner), e2, tn, preferred_element_type=F32
-    )
-    products = jnp.concatenate([g_in, g_out], axis=1).astype(BF16)
+    late = lax.dot_general(normed, gp, tn, preferred_element_type=F32).astype(BF16)
+    late = lax.psum_scatter(late, "wshard", scatter_dimension=0, tiled=True)
     heads = inner // HDIM
     conv_sum, head_sum = conv_g.sum(0), head_g.sum(0)
     smalls = (
@@ -519,7 +841,7 @@
         head_sum[:3, :heads],
         dgain.sum(0)[0],
     )
-    return grad_u, products, smalls
+    return grad_u, (early, late), smalls
 
 
 def body(
@@ -538,15 +860,16 @@
 
     def pack(which):
         out_rows = wo.reshape(2, wo.shape[0] // 2, wo.shape[1])
-        return jnp.concatenate(
+        x_part = jnp.concatenate(
             [
-                half(wi[:, :full], which),
                 half(wi[:, full:bc_at], which),
                 wi[:, bc_at:dt_at],
-                half(wi[:, dt_at:], which),
+                jnp.pad(half(wi[:, dt_at:], which), ((0, 0), (0, LANE - head_count // 2))),
             ],
             axis=1,
-        ), lax.dynamic_index_in_dim(out_rows, which, 0, keepdims=False)
+        )
+        out_part = lax.dynamic_index_in_dim(out_rows, which, 0, keepdims=False)
+        return x_part, half(wi[:, :full], which), out_part
 
     own, sent = pack(core), pack(1 - core)
     came = jax.tree.map(swap, sent)
@@ -556,10 +879,11 @@
 
     def params(layer):
         mine = core == layer
-        w_in = jnp.where(mine, own[0], came[0])
-        w_out = jnp.where(mine, own[1], came[1])
-        w_in = lax.all_gather(w_in, "wshard", axis=0, tiled=True)
-        w_out = lax.all_gather(w_out, "wshard", axis=0, tiled=True)
+        w = tuple(jnp.where(mine, a, b) for a, b in zip(own, came))
+        if layer == 0:
+            w = spread_weights(*w)
+        else:
+            w = tuple(lax.all_gather(a, "wshard", axis=0, tiled=True) for a in w)
         v = jnp.where(mine, flat, flat_other)
         parts, at = [], 0
         for a in sizes:
@@ -574,7 +898,7 @@
         hp = jnp.stack([half(a, core) for a in (dtb, al, ds)])
         hp = jnp.pad(hp, ((0, 5), (0, LANE - hp.shape[1])))
         cw = jnp.pad(channels(cw), ((0, 8 - taps), (0, 0)))
-        return w_in, w_out, (
+        return w, (
             gain_in[None],
             cw,
             channels(cb)[None],
@@ -582,77 +906,49 @@
             half(gain_out, core)[None],
         )
 
-    w_in0, w_out0, p0 = params(0)
-    w_in1, w_out1, p1 = params(1)
-    first, kept0 = forward(hidden, w_in0, w_out0, p0)
-    second, kept1 = forward(first, w_in1, w_out1, p1)
+    w0, p0 = params(0)
+    w1, p1 = params(1)
+    first, kept0 = forward(hidden, w0, p0)
+    second, kept1 = forward(first, w1, p1)
     layer_out = jnp.where(core == 0, first, second)[None]
-    grad1, products1, smalls1 = backward(out_grad, kept1, w_in1, w_out1, p1)
+    grad1, products1, smalls1 = backward(out_grad, kept1, w1, p1)
     passed = grad1.astype(BF16)
-    grad0, products0, smalls0 = backward(passed, kept0, w_in0, w_out0, p0)
+    grad0, products0, smalls0 = backward(passed, kept0, w0, p0)
     section_grad = jnp.where(core == 0, grad0, passed.astype(F32))[None]
 
-    columns = products0.shape[1]
-
-    def owned(products):
-        part = lax.psum_scatter(products, "wshard", scatter_dimension=0, tiled=True)
-        part = part.astype(BF16)
-        return part
-
-    seq_count = lax.axis_size("seq")
-    rows = width // lax.axis_size("wshard") // seq_count
-    both = jnp.concatenate(
-        [owned(p).reshape(seq_count, rows, columns) for p in (products0, products1)], axis=1
-    )
-    moved = exchange(both)
-    piece = moved.astype(F32).sum(0).astype(BF16).reshape(2, rows, columns)
-    mine = lax.dynamic_index_in_dim(piece, core, 0, keepdims=False)
-    other = swap(lax.dynamic_index_in_dim(piece, 1 - core, 0, keepdims=False))
-    inner = full // 2
-    at = (0, inner, 2 * inner, 2 * inner + (dt_at - bc_at), columns - width, columns)
-    cut_mine = [mine[:, a:b] for a, b in zip(at, at[1:])]
-    cut_other = [other[:, a:b] for a, b in zip(at, at[1:])]
-    zg, xg, dg = (whole(cut_mine[n], cut_other[n], core) for n in (0, 1, 3))
-    bcg = (cut_mine[2].astype(F32) + cut_other[2].astype(F32)).astype(BF16)
-    low_half = jnp.where(core == 0, cut_mine[4], cut_other[4])
-    high_half = jnp.where(core == 0, cut_other[4], cut_mine[4])
-    ready = jnp.concatenate([zg, xg, bcg, dg, low_half, high_half], axis=1)
-    everyone = lax.all_gather(ready, "seq", axis=0, tiled=True)
-    grad_w_in = everyone[:, :proj].astype(F32)
-    grad_w_out = jnp.concatenate(
-        [everyone[:, proj : proj + width], everyone[:, proj + width :]], axis=0
-    ).astype(F32)
-
-    small_mine = jax.tree.map(lambda a, b: jnp.where(core == 0, a, b), smalls0, smalls1)
-    small_send = jax.tree.map(lambda a, b: jnp.where(core == 0, b, a), smalls0, smalls1)
-    shapes = [a.shape for a in small_send]
-    flat_send = swap(jnp.concatenate([a.reshape(-1) for a in small_send]))
-    small_other, pos = [], 0
-    for shape in shapes:
-        count = 1
-        for n in shape:
-            count *= n
-        small_other.append(flat_send[pos : pos + count].reshape(shape))
-        pos += count
+    flat = [jnp.concatenate([a.reshape(-1) for a in g]) for g in (smalls0, smalls1)]
+    count = flat[0].size
+    block = 8 * LANE
+    flat = [jnp.pad(v, (0, 16 * block - count)).reshape(4, 4, 8, LANE) for v in flat]
+    rows = width // 64
+
+    def blocks(a):
+        return a.reshape(4, 4, rows, a.shape[1])
+
+    grids = [blocks(a) for a in products0 + products1]
+    mine, other = reduce_all(grids, jnp.stack(flat))
+    (early, late, small_mine), (early_o, late_o, small_o) = mine, other
+    grad_w_in, grad_w_out = assemble(core, early, late, early_o, late_o, proj, head_count)
+    grad_w_out = grad_w_out.reshape(-1, width)
+
+    def unflatten(v):
+        parts, pos = [], 0
+        for a in smalls0:
+            parts.append(v.reshape(-1)[pos : pos + a.size].reshape(a.shape))
+            pos += a.size
+        return parts
+
+    small_mine, small_o = unflatten(small_mine), unflatten(small_o)
     vector = jnp.concatenate(
         [
             small_mine[0],
             jnp.concatenate(
-                [
-                    whole(small_mine[1], small_other[1], core),
-                    small_mine[2] + small_other[2],
-                ],
-                axis=1,
+                [whole(small_mine[1], small_o[1], core), small_mine[2] + small_o[2]], axis=1
             ).reshape(-1),
-            whole(small_mine[3], small_other[3], core).reshape(-1),
-            whole(small_mine[4], small_other[4], core),
+            whole(small_mine[3], small_o[3], core).reshape(-1),
+            whole(small_mine[4], small_o[4], core),
         ]
     )
-    share = -(-vector.size // (seq_count * 1024)) * 1024
-    vector = jnp.pad(vector, (0, seq_count * share - vector.size)).reshape(seq_count, share)
-    part = exchange(vector).sum(0)
-    parts = lax.all_gather(part, ("seq", "wshard"), axis=0)
-    vector = parts.reshape(seq_count, -1, share).sum(1).reshape(-1)
     chan = full + dt_at - bc_at
     cuts = (width, taps * chan, chan, head_count, head_count, head_count, full)
     small, pos = [], 0

time: 752 us -> 492 us (0.65)
  the two profiles are of different devices: /device:TPU:0 before, /device:TPU:1 now
where the time goes in v2:
time: 492 us; the launch traced here: 482 us
  Pallas kernels  249 us (51%)
  waiting for transfers between devices  71.8 us (15%)
  local copies, waits for them, and re-layouts  53.4 us (11%)
  starting transfers between devices  37.3 us (8%)
  matrix products  27.9 us (6%)
  other arithmetic  26.1 us (5%)
  between operations  16.7 us (3%)
    pallas_call x4, Pallas kernels, scan_chunks(): pl.pallas_call(functools.partial(scan_kernel, reverse, decay is None), ou...  83 us
    pallas_call x1, Pallas kernels, reduce_all(): pl.pallas_call(reduce_kernel, out_shape=full + full, in_specs=[place] * 5...  65.3 us
    reduce_scatter x2, waiting for transfers between devices, backward(): late = lax.psum_scatter(late, 'wshard', scatter_dimension=0, tiled=True)  56 us
    pallas_call x1, Pallas kernels, spread_weights(): pl.pallas_call(spread_kernel, out_shape=[sds((4,) + a.shape, BF16) for a...  49.7 us
    pallas_call x14, Pallas kernels, run(): pl.pallas_call(kernel, grid=(2,), in_specs=[(same if n in shared else per...  48.8 us
    unnamed x248, local copies, waits for them, and re-layouts  31.5 us
    ppermute x10, starting transfers between devices, swap(): return lax.ppermute(x, 'section', [(0, 1), (1, 0)])  17.6 us
    reduce_scatter x2, starting transfers between devices, backward(): early = lax.psum_scatter(early, 'wshard', scatter_dimension=0, tiled=True)  10.8 us
  transfers between devices with their start and end apart: 21, of which 10 were waited for; matrix products, arithmetic and copies ran while one was open for 10% of the time, Pallas kernels for 37%

profile of v2, /device:TPU:1, one launch (start us, length us, event | category | flops | bytes accessed | tf_op | source)
XLA Modules:
  0.0 482.2 jit_solution(15336149315456751940)
XLA Ops:
  28.1 49.7 %shard_map.194 = (bf16[4,4,4,16,1408]{4,3,2,1,0:T(8,128)(2,1)S(1)}, bf16[4,4,4,16,1024]{4,3,2,1,0:T(8,128)(2,1)S(1)}, bf16[4,4,4,16,1024]{4,3,2,1,0:T(8,128)(2,1)S(1)}) custom-call(bf16[4,4,16,1408]{3,2,1,0:T(8,128)(2,1)S(1)} %bitcast.182, bf16[4,4,16,1024]{3,2,1,0:T(8,128)(2,1)S(1)} %bitcast.185, bf16[4,4,16,1024]{3,2,1,0:T(8,128)(2,1)S(1)} %bitcast.187), custom_call_target="tpu_custom_call" | custom-call | tf_op jit(solution)/shard_map/pallas_call | solution.py:568
  78.8 3.1 collective-permute-start.4
  83.4 3.0 shard_map.195
  86.4 20.7 %shard_map.197 = (f32[16,128]{1,0:T(8,128)S(1)}, bf16[16,128,128]{2,1,0:T(8,128)(2,1)S(1)}) custom-call(bf16[16,144,128]{2,1,0:T(8,128)(2,1)S(1)} %get-tuple-element.68.pieces_ref), custom_call_target="tpu_custom_call" | custom-call | tf_op jit(solution)/shard_map/pallas_call | solution.py:424
  111.5 6.9 %collective-permute-start.6 = (bf16[2,128,1024]{2,1,0:T(8,128)(2,1)S(1)}, bf16[2,128,1024]{2,1,0:T(8,128)(2,1)S(1)}, u32[]{:S(2)}, u32[]{:S(2)}) collective-permute-start(bf16[2,128,1024]{2,1,0:T(8,128)(2,1)S(1)} %bitcast.223), channel_id=1, source_target_pairs={{0,64},{64,0},{1,65},{65,1},{2,66},{66,2},{3,67},{67,3},{4,68},{68... | collective-permute-start | bytes 1572872 | tf_op jit(solution)/shard_map/ppermute | solution.py:26
  121.9 2.9 convolution_convert_fusion
  124.9 2.6 collective-permute-start.7
  131.4 3.0 shard_map.199
  134.4 19.6 %shard_map.201 = (f32[16,128]{1,0:T(8,128)S(1)}, bf16[16,128,128]{2,1,0:T(8,128)(2,1)S(1)}) custom-call(bf16[16,144,128]{2,1,0:T(8,128)(2,1)S(1)} %get-tuple-element.77.pieces_ref), custom_call_target="tpu_custom_call" | custom-call | tf_op jit(solution)/shard_map/pallas_call | solution.py:424
  159.5 2.6 convolution_convert_fusion.2
  162.2 3.2 collective-permute-start.9
  176.1 2.6 shard_map.203
  183.5 10.8 %reduce-scatter.5.cloned.1.call-start = ((), (), s32[]{:S(2)}) async-start(), calls=%async_computation.7 | async-start | bytes 5242880 | tf_op jit(solution)/shard_map/reduce_scatter | solution.py:791
  195.4 3.5 shard_map.204
  198.9 21.4 %shard_map.205.grad = bf16[16,128,128]{2,1,0:T(8,128)(2,1)S(1)} custom-call(bf16[16,128,128]{2,1,0:T(8,128)(2,1)S(1)} %copy-done.50, f32[16,128]{1,0:T(8,128)S(1)} %copy-done.72), custom_call_target="tpu_custom_call" | custom-call | tf_op jit(solution)/shard_map/pallas_call | solution.py:424
  220.4 10.6 %shard_map.206 = (f32[2,128,1280]{2,1,0:T(8,128)S(1)}, bf16[2,128,128]{2,1,0:T(8,128)(2,1)S(1)}, f32[2,8,1280]{2,1,0:T(8,128)S(1)}, f32[2,8,128]{2,1,0:T(8,128)S(1)}) custom-call(bf16[2,128,1408]{2,1,0:T(8,128)(2,1)S(1)} %bitcast.179, bf16[2,16,1280]{2,1,0:T(8,128)(2,1)S(1)} %copy-done.54, f32[8,1280]{1,0:T(8,128)S(1)} %copy-done.42, ...), custom_call_target="tpu_custom_call" | custom-call | tf_op jit(solution)/shard_map/pallas_call | solution.py:402
  232.3 3.9 collective-permute-done.10.after
  247.7 2.6 fusion.58.gr
  250.4 2.7 shard_map.208
  259.6 2.6 bitcast_convert_fusion
  263.3 3.4 shard_map.209
  266.8 21.3 %shard_map.210.grad = bf16[16,128,128]{2,1,0:T(8,128)(2,1)S(1)} custom-call(bf16[16,128,128]{2,1,0:T(8,128)(2,1)S(1)} %copy-done.48, f32[16,128]{1,0:T(8,128)S(1)} %copy-done.70), custom_call_target="tpu_custom_call" | custom-call | tf_op jit(solution)/shard_map/pallas_call | solution.py:424
  288.1 10.6 %shard_map.211 = (f32[2,128,1280]{2,1,0:T(8,128)S(1)}, bf16[2,128,128]{2,1,0:T(8,128)(2,1)S(1)}, f32[2,8,1280]{2,1,0:T(8,128)S(1)}, f32[2,8,128]{2,1,0:T(8,128)S(1)}) custom-call(bf16[2,128,1408]{2,1,0:T(8,128)(2,1)S(1)} %bitcast.176, bf16[2,16,1280]{2,1,0:T(8,128)(2,1)S(1)} %copy-done.52, f32[8,1280]{1,0:T(8,128)S(1)} %copy-done.40, ...), custom_call_target="tpu_custom_call" | custom-call | tf_op jit(solution)/shard_map/pallas_call | solution.py:402
  300.8 3.9 collective-permute-done.12.after
  305.8 2.7 bitcast_convert_fusion.1
  312.2 3.0 collective-permute-start.13
  324.1 17.7 %reduce-scatter.11.cloned.1.call-done = bf16[256,1408]{1,0:T(8,128)(2,1)} async-done(((bf16[1024,1408]{1,0:T(8,128)(2,1)}), bf16[256,1408]{1,0:T(8,128)(2,1)}) %reduce-scatter.11.cloned.1.call-update) | async-done | bytes 720912 | tf_op jit(solution)/shard_map/reduce_scatter | solution.py:834
  341.8 38.3 %reduce-scatter.7.cloned.1.call-done = bf16[256,1408]{1,0:T(8,128)(2,1)} async-done(((bf16[1024,1408]{1,0:T(8,128)(2,1)}), bf16[256,1408]{1,0:T(8,128)(2,1)}) %reduce-scatter.7.cloned.1.call-update) | async-done | bytes 720912 | tf_op jit(solution)/shard_map/reduce_scatter | solution.py:834
  382.3 65.3 %shard_map.213 = (bf16[4,4,16,2048]{3,2,1,0:T(8,128)(2,1)S(1)}, bf16[4,4,16,1408]{3,2,1,0:T(8,128)(2,1)S(1)}, f32[4,4,8,128]{3,2,1,0:T(8,128)S(1)}, bf16[4,4,16,...) custom-call(bf16[4,4,16,2048]{3,2,1,0:T(8,128)(2,1)S(1)} %bitcast.173, ...), custom_call_target="tpu_custom_call" | custom-call | tf_op jit(solution)/shard_map/pallas_call | solution.py:689
  450.3 4.0 slice.300
  454.4 4.0 slice.302
  469.1 5.9 %copy.67 = f32[1,256,4384]{1,2,0:T(8,128)} copy(f32[1,256,4384]{2,1,0:T(8,128)} %bitcast.171) | data formatting | bytes 8978432
  (453 shorter events, 107.4 us)
Async XLA Ops:
  7.2 114.7 %all-gather.4.cloned.1.call-start = ((), (), s32[]{:S(2)}) async-start(), calls=%async_computation.4 | async-start | bytes 3604480 | tf_op jit(solution)/shard_map/all_gather | solution.py:886
  11.2 3.5 collective-permute-start.1
  16.9 110.6 %all-gather.6.cloned.1.call-start = ((), (), s32[]{:S(2)}) async-start(), calls=%async_computation.5 | async-start | bytes 2621440 | tf_op jit(solution)/shard_map/all_gather | solution.py:886
  17.2 2.1 collective-permute-start.2
  21.3 138.2 %all-gather.8.cloned.1.call-start = ((), (), s32[]{:S(2)}) async-start(), calls=%async_computation.6 | async-start | bytes 2621440 | tf_op jit(solution)/shard_map/all_gather | solution.py:886
  21.4 4.2 collective-permute-start.3
  22.1 1.4 collective-permute-start
  23.7 85.0 %copy-start.65 = (f32[4,1,256]{2,1,0:T(1,128)}, f32[4,1,256]{2,1,0:T(1,128)S(1)}, u32[]{:S(2)}) copy-start(f32[4,1,256]{2,1,0:T(1,128)S(1)} %constant_dynamic-slice_fusion.5) | copy-start | bytes 12292
  23.9 131.7 %copy-start.67 = (f32[4,1,256]{2,1,0:T(1,128)}, f32[4,1,256]{2,1,0:T(1,128)S(1)}, u32[]{:S(2)}) copy-start(f32[4,1,256]{2,1,0:T(1,128)S(1)} %constant_dynamic-slice_fusion) | copy-start | bytes 12292
  25.4 57.9 %copy-start.39 = (f32[8,1280]{1,0:T(8,128)}, f32[8,1280]{1,0:T(8,128)S(1)}, u32[]{:S(2)}) copy-start(f32[8,1280]{1,0:T(8,128)S(1)} %select_maximum_fusion.1.cw) | copy-start | bytes 122884
  25.6 56.3 %copy-start.83 = (bf16[2,128,1024]{2,1,0:T(8,128)(2,1)}, bf16[2,128,1024]{2,1,0:T(8,128)(2,1)S(1)}, u32[]{:S(2)}) copy-start(bf16[2,128,1024]{2,1,0:T(8,128)(2,1)S(1)} %fusion.17) | copy-start | bytes 1572868
  28.0 293.1 %reduce-scatter.9.cloned.1.call-start = ((), (), s32[]{:S(2)}) async-start(), calls=%async_computation.9 | async-start | bytes 5242880 | tf_op jit(solution)/shard_map/reduce_scatter | solution.py:791
  77.7 30.9 %copy-start.75 = (bf16[4,4,4,16,1408]{4,3,2,1,0:T(8,128)(2,1)}, bf16[4,4,4,16,1408]{4,3,2,1,0:T(8,128)(2,1)S(1)}, u32[]{:S(2)}) copy-start(bf16[4,4,4,16,1408]{4,3,2,1,0:T(8,128)(2,1)S(1)} %get-tuple-element.64) | copy-start | bytes 8650756
  77.8 33.0 %copy-start.13 = (bf16[4,4,4,16,1024]{4,3,2,1,0:T(8,128)(2,1)}, bf16[4,4,4,16,1024]{4,3,2,1,0:T(8,128)(2,1)S(1)}, u32[]{:S(2)}) copy-start(bf16[4,4,4,16,1024]{4,3,2,1,0:T(8,128)(2,1)S(1)} %get-tuple-element.73) | copy-start | bytes 6291460
  78.8 4.6 collective-permute-start.4
  82.6 28.1 %copy-start = (f32[2,128,1024]{2,1,0:T(8,128)}, f32[2,128,1024]{2,1,0:T(8,128)S(1)}, u32[]{:S(2)}) copy-start(f32[2,128,1024]{2,1,0:T(8,128)S(1)} %fusion.55.z) | copy-start | bytes 3145732
  83.4 27.4 %copy-start.51 = (bf16[2,16,1280]{2,1,0:T(8,128)(2,1)}, bf16[2,16,1280]{2,1,0:T(8,128)(2,1)S(1)}, u32[]{:S(2)}) copy-start(bf16[2,16,1280]{2,1,0:T(8,128)(2,1)S(1)} %collective-permute-done.4.halo) | copy-start | bytes 245764
  111.5 9.3 %collective-permute-start.6 = (bf16[2,128,1024]{2,1,0:T(8,128)(2,1)S(1)}, bf16[2,128,1024]{2,1,0:T(8,128)(2,1)S(1)}, u32[]{:S(2)}, u32[]{:S(2)}) collective-permute-start(bf16[2,128,1024]{2,1,0:T(8,128)(2,1)S(1)} %bitcast.223), channel_id=1, source_target_pairs={{0,64},{64,0},{1,65},{65,1},{2,66},{66,2},{3,67},{67,3},{4,68},{68... | collective-permute-start | bytes 1572872 | tf_op jit(solution)/shard_map/ppermute | solution.py:26
  118.4 1.7 collective-permute-start.5
  124.9 5.0 %collective-permute-start.7 = (bf16[2,16,1280]{2,1,0:T(8,128)(2,1)S(1)}, bf16[2,16,1280]{2,1,0:T(8,128)(2,1)S(1)}, u32[]{:S(2)}, u32[]{:S(2)}) collective-permute-start(bf16[2,16,1280]{2,1,0:T(8,128)(2,1)S(1)} %slice.325), channel_id=1, source_target_pairs={{0,4},{4,8},{8,12},{12,16},{16,20},{20,24},{24,28},{28,32},{32,36}... | collective-permute-start | bytes 245768 | tf_op jit(solution)/shard_map/ppermute | solution.py:22
  131.4 26.4 %copy-start.53 = (bf16[2,16,1280]{2,1,0:T(8,128)(2,1)}, bf16[2,16,1280]{2,1,0:T(8,128)(2,1)S(1)}, u32[]{:S(2)}) copy-start(bf16[2,16,1280]{2,1,0:T(8,128)(2,1)S(1)} %collective-permute-done.7.halo) | copy-start | bytes 245764
  162.2 6.2 %collective-permute-start.9 = (bf16[2,128,1024]{2,1,0:T(8,128)(2,1)S(1)}, bf16[2,128,1024]{2,1,0:T(8,128)(2,1)S(1)}, u32[]{:S(2)}, u32[]{:S(2)}) collective-permute-start(bf16[2,128,1024]{2,1,0:T(8,128)(2,1)S(1)} %bitcast.221), channel_id=1, source_target_pairs={{0,64},{64,0},{1,65},{65,1},{2,66},{66,2},{3,67},{67,3},{4,68},{68... | collective-permute-start | bytes 1572872 | tf_op jit(solution)/shard_map/ppermute | solution.py:26
  165.3 1.8 collective-permute-start.8
  183.5 139.1 %reduce-scatter.5.cloned.1.call-start = ((), (), s32[]{:S(2)}) async-start(), calls=%async_computation.7 | async-start | bytes 5242880 | tf_op jit(solution)/shard_map/reduce_scatter | solution.py:791
  194.3 26.0 %copy-start.12 = (bf16[256,1408]{1,0:T(8,128)(2,1)S(1)}, bf16[256,1408]{1,0:T(8,128)(2,1)}, u32[]{:S(2)}) copy-start(bf16[256,1408]{1,0:T(8,128)(2,1)} %copy-done.10) | copy-start | bytes 2162692
  194.3 26.0 %copy-start.21 = (bf16[16,128,128]{2,1,0:T(8,128)(2,1)S(1)}, bf16[16,128,128]{2,1,0:T(8,128)(2,1)}, u32[]{:S(2)}) copy-start(bf16[16,128,128]{2,1,0:T(8,128)(2,1)} %copy-done.20) | copy-start | bytes 1572868
  231.0 5.2 %collective-permute-start.10 = (f32[2,8,1280]{2,1,0:T(8,128)S(1)}, f32[2,8,1280]{2,1,0:T(8,128)S(1)}, u32[]{:S(2)}, u32[]{:S(2)}) collective-permute-start(f32[2,8,1280]{2,1,0:T(8,128)S(1)} %slice.279), channel_id=1, source_target_pairs={{4,0},{8,4},{12,8},{16,12},{20,16},{24,20},{28,24},{32,28},{36,32}... | collective-permute-start | bytes 245768 | tf_op jit(solution)/shard_map/ppermute | solution.py:22
  239.9 3.4 collective-permute-start.11
  258.6 83.2 %reduce-scatter.11.cloned.1.call-start = ((), (), s32[]{:S(2)}) async-start(), calls=%async_computation.10 | async-start | bytes 3604480 | tf_op jit(solution)/shard_map/reduce_scatter | solution.py:834
  262.3 117.7 %reduce-scatter.7.cloned.1.call-start = ((), (), s32[]{:S(2)}) async-start(), calls=%async_computation.8 | async-start | bytes 3604480 | tf_op jit(solution)/shard_map/reduce_scatter | solution.py:834
  299.3 5.3 %collective-permute-start.12 = (f32[2,8,1280]{2,1,0:T(8,128)S(1)}, f32[2,8,1280]{2,1,0:T(8,128)S(1)}, u32[]{:S(2)}, u32[]{:S(2)}) collective-permute-start(f32[2,8,1280]{2,1,0:T(8,128)S(1)} %slice.280), channel_id=1, source_target_pairs={{4,0},{8,4},{12,8},{16,12},{20,16},{24,20},{28,24},{32,28},{36,32}... | collective-permute-start | bytes 245768 | tf_op jit(solution)/shard_map/ppermute | solution.py:22
  312.2 5.7 %collective-permute-start.13 = (bf16[2,128,1024]{2,1,0:T(8,128)(2,1)S(1)}, bf16[2,128,1024]{2,1,0:T(8,128)(2,1)S(1)}, u32[]{:S(2)}, u32[]{:S(2)}) collective-permute-start(bf16[2,128,1024]{2,1,0:T(8,128)(2,1)S(1)} %bitcast.210), channel_id=1, source_target_pairs={{0,64},{64,0},{1,65},{65,1},{2,66},{66,2},{3,67},{67,3},{4,68},{68... | collective-permute-start | bytes 1572872 | tf_op jit(solution)/shard_map/ppermute | solution.py:26
  (111 other events, 645.0 us)
Sparse Core Ops, SparseCore 0:
  17.0 44.2 all-gather.3
  63.5 30.9 all-gather.5
  96.2 30.8 all-gather.7
  183.6 44.1 reduce-scatter.8
  258.7 44.9 reduce-scatter.4
  306.0 35.7 reduce-scatter.10
  344.2 35.8 reduce-scatter.6
